TPU v7x, 512 devices: a whole 4x8x8 slice. The times are simulated.
512 devices in a mesh: delay: 16 (over y, core), row: 32 (over z, x).
Axes of the slice: x: 4, y: 8, z: 8, core: 2. Of those that a mesh axis runs over, the one named last changes fastest.
Arguments:
- incident: bfloat16 [64, 4096], P(None, 'row'), may hold values from -12 to 12
- onset: int32 [64], replicated, may hold values from 0 to 2
- beta: float32 [4096], P('delay'), may hold values from 0.05 to 0.5
- inverse_block: bfloat16 [4096, 4096], P('row', 'delay'), may hold values from -0.0625 to 0.0625
- delay_blocks: bfloat16 [16, 4096, 4096], P('delay', None, 'row'), may hold values from -0.09375 to 0.09375
- history_sum: float32 [16, 64, 4096], P('delay', None, 'row'), may hold values from -12 to 12
Outputs:
- currents: bfloat16 [3, 64, 4096], P(None, None, 'delay')
- carried: float32 [16, 64, 4096], P('delay', None, 'row')
All inputs are finite; a program needn't handle non-finite values.
Results may differ from a plain program's by a relative error of at most 0.0056.
Values may be sent and summed in bfloat16 or wider, within the bound.
A program may use at most 64 MiB of HBM per device.

v0:
```python
import jax
import jax.numpy as jnp
from jax import lax
from jax.sharding import PartitionSpec as P

STEPS = 3


def broadcast(value, axis, root):
    return lax.dynamic_index_in_dim(lax.all_gather(value, axis), root, 0, keepdims=False)


def in_blocks(value, dim, devices):
    dims = value.shape
    blocks = value.reshape(*dims[:dim], devices, dims[dim] // devices, *dims[dim + 1 :])
    return jnp.moveaxis(blocks, dim, 0)


def sent_and_summed(value, axis, dim):
    devices = lax.axis_size(axis)
    blocks = lax.all_to_all(in_blocks(value, dim, devices), axis, 0, 0, tiled=True)
    return jnp.sum(blocks, axis=0)


def copy_for_each(value, axis):
    copies = jnp.broadcast_to(value, (lax.axis_size(axis), *value.shape))
    return lax.all_to_all(copies, axis, split_axis=0, concat_axis=0, tiled=True)


def joined_along(blocks, dim):
    blocks = jnp.moveaxis(blocks, 0, dim)
    dims = blocks.shape
    return blocks.reshape(*dims[:dim], dims[dim] * dims[dim + 1], *dims[dim + 2 :])


def gathered_copies(value, axis, dim):
    blocks = copy_for_each(value, axis)
    return joined_along(blocks, dim)


def passed_along(value, axis, by):
    devices = lax.axis_size(axis)
    pairs = [(i, i + by) for i in range(devices) if 0 <= i + by < devices]
    return lax.ppermute(value, axis, pairs)


def per_device(incident, onset, beta, inverse_block, delay_blocks, history_sum):
    future = history_sum[0]
    matrix = delay_blocks[0]
    incident_wide = incident.astype(jnp.float32)
    outputs = []
    for step_index in range(STEPS):
        offset_time = (step_index - onset).astype(jnp.float32)
        envelope = jnp.where(offset_time >= 0.0, jnp.exp(-((offset_time - 1.0) ** 2) / 4.0), 0.0)
        residual = (incident_wide * envelope[:, None] - future).astype(jnp.bfloat16)
        residual = broadcast(residual, "delay", 0)
        partial_sum = jnp.dot(residual, inverse_block, preferred_element_type=jnp.float32)
        solved = sent_and_summed(partial_sum, "row", 0)
        current = (solved / (1.0 + beta[None, :] * solved * solved)).astype(jnp.bfloat16)
        own_block = gathered_copies(current, "row", 0)
        gathered = lax.all_gather(own_block, "delay", axis=1, tiled=True)
        outputs.append(own_block)
        passed = passed_along(future, "delay", -1)
        future = passed + jnp.dot(gathered, matrix, preferred_element_type=jnp.float32)
    return (jnp.stack(outputs), future[None])


def solution(mesh):
    placed = (
        P(None, "row"),
        P(),
        P("delay"),
        P("row", "delay"),
        P("delay", None, "row"),
        P("delay", None, "row"),
    )
    return jax.shard_map(
        per_device,
        mesh=mesh,
        in_specs=placed,
        out_specs=(P(None, None, "delay"), P("delay", None, "row")),
        check_vma=False,
    )
```

profile of v0, /device:TPU:1, one launch (start us, length us, event | category | flops | bytes accessed | tf_op | source)
XLA Modules:
  0.0 199.1 jit_solution(9493592428893358727)
XLA Ops:
  0.6 0.0 copy-start
  0.6 0.8 compare_select_fusion.1
  1.4 0.9 fusion.12
  2.3 0.0 copy-start.1
  2.3 21.7 %all-gather = bf16[1024,128]{1,0:T(8,128)(2,1)S(1)} all-gather(bf16[64,128]{1,0:T(8,128)(2,1)S(1)} %fusion.12), channel_id=2, replica_groups=mesh['delay'=16,'row'=32] {'delay'}, dimensions={0}, use_global_device_ids=true | all-gather | bytes 278528 | tf_op jit(solution)/shard_map/all_gather | solution.py:10
  24.0 0.0 copy-done.1
  24.0 0.1 fusion.9
  24.1 0.1 copy.14
  24.2 19.6 %all_to_all.30 = f32[32,2,256]{2,1,0:T(2,128)S(1)} all-to-all(f32[32,2,256]{2,1,0:T(2,128)S(1)} %copy.14), channel_id=1, replica_groups=mesh['delay'=16,'row'=32] {'row'}, dimensions={0} | all-to-all | bytes 131072 | tf_op jit(solution)/shard_map/all_to_all | solution.py:21
  43.8 0.0 copy-start.4
  43.8 0.6 copy-done.4
  44.5 0.6 broadcast_in_dim.22
  45.1 0.0 copy-start.3
  45.1 4.0 %all-to-all-start.1 = ((bf16[32,2,256]{2,1,0:T(2,128)(2,1)}), bf16[32,2,256]{2,1,0:T(2,128)(2,1)S(1)}, u32[]{:S(2)}, u32[]{:S(2)}) async-start(bf16[32,2,256]{2,1,0:T(2,128)(2,1)} %broadcast_in_dim.22), calls=%async_computation.1 | async-start | bytes 65536 | tf_op jit(solution)/shard_map/all_to_all | solution.py:27
  49.1 0.0 copy-done.3
  49.1 3.5 %collective-permute-start = (f32[64,128]{1,0:T(8,128)S(1)}, f32[64,128]{1,0:T(8,128)S(1)}, u32[]{:S(2)}, u32[]{:S(2)}) collective-permute-start(f32[64,128]{1,0:T(8,128)S(1)} %bitcast.29), channel_id=1, source_target_pairs={{32,0},{64,32},{96,64},{128,96},{160,128},{192,160},{224,192},{256... | collective-permute-start | bytes 98312 | tf_op jit(solution)/shard_map/ppermute | solution.py:44
  52.6 5.1 %all-to-all-done.1 = bf16[32,2,256]{2,1,0:T(2,128)(2,1)S(1)} async-done(((bf16[32,2,256]{2,1,0:T(2,128)(2,1)}), bf16[32,2,256]{2,1,0:T(2,128)(2,1)S(1)}, u32[]{:S(2)}, u32[]{:S(2)}) %all-to-all-start.1) | async-done | bytes 32800 | tf_op jit(solution)/shard_map/all_to_all | solution.py:27
  57.7 0.0 copy-start.2
  57.8 18.9 %all_gather.29 = bf16[64,4096]{1,0:T(8,128)(2,1)S(1)} all-gather(bf16[64,256]{1,0:T(8,128)(2,1)S(1)} %reshape.26), channel_id=1, replica_groups=mesh['delay'=16,'row'=32] {'delay'}, dimensions={1}, use_global_device_ids=true | all-gather | bytes 557056 | tf_op jit(solution)/shard_map/all_gather | solution.py:61
  76.7 0.0 collective-permute-done
  76.7 0.0 copy-done
  76.7 0.0 copy-done.2
  76.7 0.3 fusion.14
  77.0 16.0 %all-gather.1 = bf16[1024,128]{1,0:T(8,128)(2,1)S(1)} all-gather(bf16[64,128]{1,0:T(8,128)(2,1)S(1)} %get-tuple-element.7), channel_id=3, replica_groups=mesh['delay'=16,'row'=32] {'delay'}, dimensions={0}, use_global_device_ids=true | all-gather | bytes 278528 | tf_op jit(solution)/shard_map/all_gather | solution.py:10
  93.1 0.1 fusion.7
  93.2 0.1 copy.16
  93.3 11.8 %all_to_all.31 = f32[32,2,256]{2,1,0:T(2,128)S(1)} all-to-all(f32[32,2,256]{2,1,0:T(2,128)S(1)} %copy.16), channel_id=1, replica_groups=mesh['delay'=16,'row'=32] {'row'}, dimensions={0} | all-to-all | bytes 131072 | tf_op jit(solution)/shard_map/all_to_all | solution.py:21
  105.2 0.6 broadcast_in_dim.23
  105.8 3.9 %all-to-all-start.3 = ((bf16[32,2,256]{2,1,0:T(2,128)(2,1)}), bf16[32,2,256]{2,1,0:T(2,128)(2,1)S(1)}, u32[]{:S(2)}, u32[]{:S(2)}) async-start(bf16[32,2,256]{2,1,0:T(2,128)(2,1)} %broadcast_in_dim.23), calls=%async_computation.3 | async-start | bytes 65536 | tf_op jit(solution)/shard_map/all_to_all | solution.py:27
  109.7 3.3 %collective-permute-start.1 = (f32[64,128]{1,0:T(8,128)S(1)}, f32[64,128]{1,0:T(8,128)S(1)}, u32[]{:S(2)}, u32[]{:S(2)}) collective-permute-start(f32[64,128]{1,0:T(8,128)S(1)} %get-tuple-element.8), channel_id=1, source_target_pairs={{32,0},{64,32},{96,64},{128,96},{160,128},{192,160},{224,192},{256... | collective-permute-start | bytes 98312 | tf_op jit(solution)/shard_map/ppermute | solution.py:44
  113.0 5.3 %all-to-all-done.3 = bf16[32,2,256]{2,1,0:T(2,128)(2,1)S(1)} async-done(((bf16[32,2,256]{2,1,0:T(2,128)(2,1)}), bf16[32,2,256]{2,1,0:T(2,128)(2,1)S(1)}, u32[]{:S(2)}, u32[]{:S(2)}) %all-to-all-start.3) | async-done | bytes 32800 | tf_op jit(solution)/shard_map/all_to_all | solution.py:27
  118.3 18.7 %all_gather.32 = bf16[64,4096]{1,0:T(8,128)(2,1)S(1)} all-gather(bf16[64,256]{1,0:T(8,128)(2,1)S(1)} %reshape.27), channel_id=1, replica_groups=mesh['delay'=16,'row'=32] {'delay'}, dimensions={1}, use_global_device_ids=true | all-gather | bytes 557056 | tf_op jit(solution)/shard_map/all_gather | solution.py:61
  137.0 0.3 fusion.2
  137.4 0.0 collective-permute-done.1
  137.4 0.1 fusion.16
  137.5 16.0 %all-gather.2 = bf16[1024,128]{1,0:T(8,128)(2,1)S(1)} all-gather(bf16[64,128]{1,0:T(8,128)(2,1)S(1)} %get-tuple-element.2), channel_id=4, replica_groups=mesh['delay'=16,'row'=32] {'delay'}, dimensions={0}, use_global_device_ids=true | all-gather | bytes 278528 | tf_op jit(solution)/shard_map/all_gather | solution.py:10
  153.5 0.1 fusion.5
  153.6 0.1 copy.18
  153.7 11.8 %all_to_all.32 = f32[32,2,256]{2,1,0:T(2,128)S(1)} all-to-all(f32[32,2,256]{2,1,0:T(2,128)S(1)} %copy.18), channel_id=1, replica_groups=mesh['delay'=16,'row'=32] {'row'}, dimensions={0} | all-to-all | bytes 131072 | tf_op jit(solution)/shard_map/all_to_all | solution.py:21
  165.6 0.6 broadcast_in_dim.24
  166.2 3.9 %all-to-all-start.5 = ((bf16[32,2,256]{2,1,0:T(2,128)(2,1)}), bf16[32,2,256]{2,1,0:T(2,128)(2,1)S(1)}, u32[]{:S(2)}, u32[]{:S(2)}) async-start(bf16[32,2,256]{2,1,0:T(2,128)(2,1)} %broadcast_in_dim.24), calls=%async_computation.5 | async-start | bytes 65536 | tf_op jit(solution)/shard_map/all_to_all | solution.py:27
  170.1 3.3 %collective-permute-start.2 = (f32[64,128]{1,0:T(8,128)S(1)}, f32[64,128]{1,0:T(8,128)S(1)}, u32[]{:S(2)}, u32[]{:S(2)}) collective-permute-start(f32[64,128]{1,0:T(8,128)S(1)} %get-tuple-element.3), channel_id=1, source_target_pairs={{32,0},{64,32},{96,64},{128,96},{160,128},{192,160},{224,192},{256... | collective-permute-start | bytes 98312 | tf_op jit(solution)/shard_map/ppermute | solution.py:44
  173.4 5.3 %all-to-all-done.5 = bf16[32,2,256]{2,1,0:T(2,128)(2,1)S(1)} async-done(((bf16[32,2,256]{2,1,0:T(2,128)(2,1)}), bf16[32,2,256]{2,1,0:T(2,128)(2,1)S(1)}, u32[]{:S(2)}, u32[]{:S(2)}) %all-to-all-start.5) | async-done | bytes 32800 | tf_op jit(solution)/shard_map/all_to_all | solution.py:27
  178.7 18.7 %all_gather.35 = bf16[64,4096]{1,0:T(8,128)(2,1)S(1)} all-gather(bf16[64,256]{1,0:T(8,128)(2,1)S(1)} %reshape.28), channel_id=1, replica_groups=mesh['delay'=16,'row'=32] {'delay'}, dimensions={1}, use_global_device_ids=true | all-gather | bytes 557056 | tf_op jit(solution)/shard_map/all_gather | solution.py:61
  197.5 0.3 fusion
  197.8 0.7 pad_maximum_fusion
  198.5 0.0 collective-permute-done.2
  198.5 0.6 add_bitcast_fusion
  (15 shorter events, 0.3 us)
Async XLA Ops:
  0.6 76.0 %copy-start = (bf16[1,4096,128]{2,1,0:T(8,128)(2,1)S(1)}, bf16[1,4096,128]{2,1,0:T(8,128)(2,1)}, u32[]{:S(2)}) copy-start(bf16[1,4096,128]{2,1,0:T(8,128)(2,1)} %param.10) | copy-start | bytes 3145732
  2.3 21.7 %copy-start.1 = (bf16[128,256]{1,0:T(8,128)(2,1)S(1)}, bf16[128,256]{1,0:T(8,128)(2,1)}, u32[]{:S(2)}) copy-start(bf16[128,256]{1,0:T(8,128)(2,1)} %param.9) | copy-start | bytes 196612
  43.8 0.7 copy-start.4
  45.1 4.0 %copy-start.3 = (f32[1,64,128]{2,1,0:T(8,128)S(1)}, f32[1,64,128]{2,1,0:T(8,128)}, u32[]{:S(2)}) copy-start(f32[1,64,128]{2,1,0:T(8,128)} %param.11) | copy-start | bytes 98308
  45.1 12.6 %all-to-all-start.1 = ((bf16[32,2,256]{2,1,0:T(2,128)(2,1)}), bf16[32,2,256]{2,1,0:T(2,128)(2,1)S(1)}, u32[]{:S(2)}, u32[]{:S(2)}) async-start(bf16[32,2,256]{2,1,0:T(2,128)(2,1)} %broadcast_in_dim.22), calls=%async_computation.1 | async-start | bytes 65536 | tf_op jit(solution)/shard_map/all_to_all | solution.py:27
  49.1 27.6 %collective-permute-start = (f32[64,128]{1,0:T(8,128)S(1)}, f32[64,128]{1,0:T(8,128)S(1)}, u32[]{:S(2)}, u32[]{:S(2)}) collective-permute-start(f32[64,128]{1,0:T(8,128)S(1)} %bitcast.29), channel_id=1, source_target_pairs={{32,0},{64,32},{96,64},{128,96},{160,128},{192,160},{224,192},{256... | collective-permute-start | bytes 98312 | tf_op jit(solution)/shard_map/ppermute | solution.py:44
  57.7 18.9 %copy-start.2 = (bf16[64,128]{1,0:T(8,128)(2,1)S(1)}, bf16[64,128]{1,0:T(8,128)(2,1)}, u32[]{:S(2)}) copy-start(bf16[64,128]{1,0:T(8,128)(2,1)} %param.6) | copy-start | bytes 49156
  105.8 12.5 %all-to-all-start.3 = ((bf16[32,2,256]{2,1,0:T(2,128)(2,1)}), bf16[32,2,256]{2,1,0:T(2,128)(2,1)S(1)}, u32[]{:S(2)}, u32[]{:S(2)}) async-start(bf16[32,2,256]{2,1,0:T(2,128)(2,1)} %broadcast_in_dim.23), calls=%async_computation.3 | async-start | bytes 65536 | tf_op jit(solution)/shard_map/all_to_all | solution.py:27
  109.7 27.7 %collective-permute-start.1 = (f32[64,128]{1,0:T(8,128)S(1)}, f32[64,128]{1,0:T(8,128)S(1)}, u32[]{:S(2)}, u32[]{:S(2)}) collective-permute-start(f32[64,128]{1,0:T(8,128)S(1)} %get-tuple-element.8), channel_id=1, source_target_pairs={{32,0},{64,32},{96,64},{128,96},{160,128},{192,160},{224,192},{256... | collective-permute-start | bytes 98312 | tf_op jit(solution)/shard_map/ppermute | solution.py:44
  166.2 12.5 %all-to-all-start.5 = ((bf16[32,2,256]{2,1,0:T(2,128)(2,1)}), bf16[32,2,256]{2,1,0:T(2,128)(2,1)S(1)}, u32[]{:S(2)}, u32[]{:S(2)}) async-start(bf16[32,2,256]{2,1,0:T(2,128)(2,1)} %broadcast_in_dim.24), calls=%async_computation.5 | async-start | bytes 65536 | tf_op jit(solution)/shard_map/all_to_all | solution.py:27
  170.1 28.4 %collective-permute-start.2 = (f32[64,128]{1,0:T(8,128)S(1)}, f32[64,128]{1,0:T(8,128)S(1)}, u32[]{:S(2)}, u32[]{:S(2)}) collective-permute-start(f32[64,128]{1,0:T(8,128)S(1)} %get-tuple-element.3), channel_id=1, source_target_pairs={{32,0},{64,32},{96,64},{128,96},{160,128},{192,160},{224,192},{256... | collective-permute-start | bytes 98312 | tf_op jit(solution)/shard_map/ppermute | solution.py:44
where the time goes:
time: 200 us; the launch traced here: 199 us
  blocking collectives  153 us (76%)
  starting transfers between devices  21.8 us (11%)
  waiting for transfers between devices  15.7 us (8%)
  other arithmetic  3.13 us (2%)
  local copies, waits for them, and re-layouts  2.87 us (1%)
    all_gather x3, blocking collectives, per_device(): gathered = lax.all_gather(own_block, 'delay', axis=1, tiled=True)  56.4 us
    all_gather x3, blocking collectives, broadcast(): lax.all_gather(value, axis)  53.8 us
    all_to_all x3, blocking collectives, sent_and_summed(): lax.all_to_all(in_blocks(value, dim, devices), axis, 0, 0, tiled=True)  43.3 us
    all_to_all x3, waiting for transfers between devices, copy_for_each(): return lax.all_to_all(copies, axis, split_axis=0, concat_axis=0, tiled=True)  15.7 us
    all_to_all x3, starting transfers between devices, copy_for_each(): return lax.all_to_all(copies, axis, split_axis=0, concat_axis=0, tiled=True)  11.7 us
    ppermute x3, starting transfers between devices, passed_along(): return lax.ppermute(value, axis, pairs)  10.1 us
  transfers between devices with their start and end apart: 6, of which 3 were waited for; matrix products, arithmetic and copies ran while one was open for 1% of the time, Pallas kernels for 0%

commit v1 on v0

v1 whole, which is shorter than its diff:
```python
import jax
import jax.numpy as jnp
from jax import lax
from jax.experimental import pallas as pl
from jax.experimental.pallas import tpu as pltpu
from jax.sharding import PartitionSpec as P

STEPS = 3
MESH = pl.DeviceIdType.MESH
F32, BF16 = jnp.float32, jnp.bfloat16
NY, NC, NZ, NX = 8, 2, 8, 4
NQ = NX * NC
ROWS = 8


def kernel(
    incident, onset, beta, inverse, matrix, history,
    currents, carried,
    inc_v, mat_v, inv_v, dl_v, stage_v, beta_v, hb_v, base_v, zbuf, xbuf, c_all, passed, future, cur_v,
    load_sem, send_sem, recv_sem, z_send, z_recv, x_send, x_recv, c_send, c_recv, p_send, p_recv, out_sem,
):
    d, r = lax.axis_index("delay"), lax.axis_index("row")
    y, c = d // NC, d % NC
    z, x = r // NX, r % NX
    q = x * NC + c
    slab = y * NQ + q

    def at(ty, tc, tz, tx):
        return (ty * NC + tc, tz * NX + tx)

    def at_slab(i):
        t = lax.rem(slab + i, NY * NQ)
        ty, tq = t // NQ, t % NQ
        return at(ty, tq % NC, z, tq // NC)

    def at_z(i):
        return at(y, c, lax.rem(z + i, NZ), x)

    def at_q(i):
        tq = lax.rem(q + i, NQ)
        return at(y, tq % NC, z, tq // NC)

    def at_x(i):
        return at(y, c, z, lax.rem(x + i, NX))

    def remote(src, dst, send, recv, target):
        return pltpu.make_async_remote_copy(
            src_ref=src, dst_ref=dst, send_sem=send, recv_sem=recv, device_id=target, device_id_type=MESH
        )

    def arrived(ref, sem):
        pltpu.make_async_copy(ref, ref, sem).wait()

    load_inc = pltpu.make_async_copy(incident, inc_v, load_sem.at[0])
    load_inc.start()
    load_mat = pltpu.make_async_copy(matrix.at[0], mat_v, load_sem.at[1])
    load_mat.start()

    barrier = pltpu.get_barrier_semaphore()

    def greet_slab(i, _):
        pl.semaphore_signal(barrier, inc=1, device_id=at_slab(i), device_id_type=MESH)
        return 0

    def greet_z(i, _):
        pl.semaphore_signal(barrier, inc=1, device_id=at_z(i), device_id_type=MESH)
        return 0

    lax.fori_loop(1, NZ, greet_z, 0)
    lax.fori_loop(1, NY * NQ, greet_slab, 0)
    pl.semaphore_wait(barrier, NZ - 1 + NY * NQ - 1)

    for s in range(STEPS):

        @pl.when(d == s)
        def _(s=s):
            def send(i, _):
                t = lax.rem(d + i, NY * NC)
                rows = pl.ds(pl.multiple_of(t // NC * ROWS, ROWS), ROWS)
                remote(history.at[0, rows], hb_v.at[s], send_sem.at[0], recv_sem.at[s], (t, r)).start()
                return 0

            lax.fori_loop(1, NY * NC, send, 0)
            own = pl.ds(pl.multiple_of(y * ROWS, ROWS), ROWS)
            pltpu.make_async_copy(history.at[0, own], hb_v.at[s], recv_sem.at[s]).start()

    qy_c, qy_x = y % NC, y // NC

    def spread(src, dst, send, recv):
        def one(i, _):
            t = lax.rem(y + i, NY)
            here = jnp.logical_and(t == y, q == y)

            @pl.when(here)
            def _():
                pltpu.make_async_copy(src, dst, recv).start()

            @pl.when(jnp.logical_not(here))
            def _():
                remote(src, dst, send, recv, at(t, qy_c, z, qy_x)).start()

            return 0

        lax.fori_loop(0, NY, one, 0)

    def spread_done(src, send):
        def one(i, _):
            @pl.when(jnp.logical_not(jnp.logical_and(i == 0, q == y)))
            def _():
                pltpu.make_async_copy(src, src, send).wait()

            return 0

        lax.fori_loop(0, NY, one, 0)

    x_rows = pl.ds(pl.multiple_of(x * 128, 128), 128)
    c_cols = pl.ds(pl.multiple_of(c * 256, 256), 256)
    spread(inverse, inv_v.at[x_rows, c_cols], send_sem.at[1], recv_sem.at[3])

    @pl.when(x == 0)
    def _():
        spread(beta, beta_v.at[c], send_sem.at[2], recv_sem.at[4])

    for k in range(2):

        @pl.when(d == k)
        def _(k=k):
            def send(i, _):
                t = lax.rem(d + i, NY * NC)
                rows = pl.ds(pl.multiple_of(t * 256, 256), 256)
                remote(matrix.at[0, rows], stage_v.at[k], send_sem.at[3], recv_sem.at[5 + k], (t, r)).start()
                return 0

            lax.fori_loop(1, NY * NC, send, 0)
            own = pl.ds(pl.multiple_of(d * 256, 256), 256)
            pltpu.make_async_copy(matrix.at[0, own], stage_v.at[k], recv_sem.at[5 + k]).start()

    def pass_on(src, k):
        @pl.when(d > 0)
        def _():
            remote(src, passed.at[k], p_send.at[k], p_recv.at[k], (jnp.maximum(d - 1, 0), r)).start()

    def take(k):
        @pl.when(d < NY * NC - 1)
        def _():
            arrived(passed.at[k], p_recv.at[k])

        return jnp.where(d < NY * NC - 1, passed[k], 0.0)

    pass_on(history.at[0], 0)

    load_inc.wait()
    future[0] = inc_v[...].astype(F32)
    own_rows = pl.ds(pl.multiple_of(y * ROWS, ROWS), ROWS)
    wide = future[0, own_rows]
    row_of = lax.broadcasted_iota(jnp.int32, (ROWS, 128), 0)
    start = jnp.zeros((ROWS, 128), jnp.int32)
    for e in range(ROWS):
        start = jnp.where(row_of == e, onset[y * ROWS + e], start)
    for s in range(STEPS):
        offset = (s - start).astype(F32)
        envelope = jnp.where(offset >= 0.0, jnp.exp(-((offset - 1.0) ** 2) / 4.0), 0.0)
        arrived(hb_v.at[s], recv_sem.at[s])
        base_v[x, s] = wide * envelope - hb_v[s]
    for i in range(1, NX):
        remote(base_v.at[x], base_v.at[x], send_sem.at[4], recv_sem.at[7], at_x(i)).start()
    arrived(base_v.at[pl.ds(0, NX - 1)], recv_sem.at[7])

    def base(s):
        return jnp.concatenate([base_v[i, s] for i in range(NX)], axis=1)

    def forward(k):
        arrived(stage_v.at[k], recv_sem.at[5 + k])
        rows = pl.ds(pl.multiple_of(c * 256, 256), 256)
        cols = pl.ds(pl.multiple_of(x * 128, 128), 128)
        spread(stage_v.at[k], dl_v.at[k, rows, cols], send_sem.at[5 + k], recv_sem.at[8 + k])

    def product(s):
        arrived(c_all.at[s, pl.ds(0, (NY * NQ - 1) * 16)], c_recv.at[s])
        total = jnp.zeros((64, 128), F32)
        for qq in range(NQ):
            block = c_all[s, pl.ds(qq * 128, 128)].astype(F32).reshape(NY, 2, ROWS, 256)
            for half in range(2):
                values = block[:, half].reshape(64, 256).astype(BF16)
                total += jnp.dot(values, mat_v[pl.ds(qq * 512 + half * 256, 256)], preferred_element_type=F32)
        block = c_all[s, pl.ds(pl.multiple_of(y * 128, 128), 128)].astype(F32).reshape(NY, 2, ROWS, 256)
        cur_v[s] = jnp.where(c == 0, block[:, 0], block[:, 1]).reshape(64, 256).astype(BF16)
        pltpu.make_async_copy(cur_v.at[s], currents.at[s], out_sem.at[s]).start()
        return total

    forward(0)
    earlier = jnp.zeros((ROWS, 512), F32)
    residual = base(0)
    for s in range(STEPS):
        if s == 0:
            arrived(inv_v, recv_sem.at[3])
        zbuf[s, z] = jnp.dot(residual.astype(BF16), inv_v[...], preferred_element_type=F32)
        for i in range(1, NZ):
            remote(zbuf.at[s, z], zbuf.at[s, z], z_send.at[s], z_recv.at[s], at_z(i)).start()
        if s == 0:
            forward(1)
            arrived(beta_v, recv_sem.at[4])
        if s == 1:
            arrived(dl_v.at[1], recv_sem.at[9])
            earlier = jnp.dot(current.astype(BF16), dl_v[1], preferred_element_type=F32)
        if s == 2:
            load_mat.wait()
            future[0] = take(0) + product(0)
            pass_on(future.at[0], 1)
        arrived(zbuf.at[s, pl.ds(0, NZ - 1)], z_recv.at[s])
        solved = zbuf[s, 0]
        for i in range(1, NZ):
            solved += zbuf[s, i]
        beta_wide = jnp.concatenate([beta_v[0], beta_v[1]], axis=1)
        current = (solved / (1.0 + beta_wide * solved * solved)).astype(BF16).astype(F32)
        mine = pl.ds(pl.multiple_of(q * 128 + y * 16, 16), 16)
        c_all[s, mine] = jnp.concatenate([current[:, :256], current[:, 256:]], axis=0).astype(BF16)
        if s < STEPS - 1:
            if s == 0:
                arrived(dl_v.at[0], recv_sem.at[8])
            xbuf[s, q] = jnp.dot(current.astype(BF16), dl_v[0], preferred_element_type=F32) + earlier
            for i in range(1, NQ):
                remote(xbuf.at[s, q], xbuf.at[s, q], x_send.at[s], x_recv.at[s], at_q(i)).start()

        def send_values(i, _):
            remote(c_all.at[s, mine], c_all.at[s, mine], c_send.at[s], c_recv.at[s], at_slab(i)).start()
            return 0

        lax.fori_loop(1, NY * NQ, send_values, 0)
        if s < STEPS - 1:
            arrived(xbuf.at[s, pl.ds(0, NQ - 1)], x_recv.at[s])
            total = xbuf[s, 0]
            for i in range(1, NQ):
                total += xbuf[s, i]
            residual = base(s + 1) - total

    future[1] = take(1) + product(1)
    pass_on(future.at[1], 2)
    future[2] = product(2)
    future[2] = future[2] + take(2)
    out = pltpu.make_async_copy(future.at[2], carried.at[0], out_sem.at[STEPS])
    out.start()

    for s in range(STEPS):
        @pl.when(d == s)
        def _():
            def one(i, _):
                pltpu.make_async_copy(hb_v.at[0], hb_v.at[0], send_sem.at[0]).wait()
                return 0

            lax.fori_loop(1, NY * NC, one, 0)

        pltpu.make_async_copy(zbuf.at[s, pl.ds(0, NZ - 1)], zbuf.at[s, pl.ds(0, NZ - 1)], z_send.at[s]).wait()
        sent = c_all.at[s, pl.ds(0, (NY * NQ - 1) * 16)]
        pltpu.make_async_copy(sent, sent, c_send.at[s]).wait()
        if s < STEPS - 1:
            sent = xbuf.at[s, pl.ds(0, NQ - 1)]
            pltpu.make_async_copy(sent, sent, x_send.at[s]).wait()

        @pl.when(d > 0)
        def _(s=s):
            pltpu.make_async_copy(passed.at[s], passed.at[s], p_send.at[s]).wait()

        pltpu.make_async_copy(cur_v.at[s], currents.at[s], out_sem.at[s]).wait()
    spread_done(inverse, send_sem.at[1])

    @pl.when(x == 0)
    def _():
        spread_done(beta, send_sem.at[2])

    for k in range(2):
        @pl.when(d == k)
        def _():
            def one(i, _):
                pltpu.make_async_copy(stage_v.at[0], stage_v.at[0], send_sem.at[3]).wait()
                return 0

            lax.fori_loop(1, NY * NC, one, 0)

        spread_done(stage_v.at[k], send_sem.at[5 + k])
    sent = base_v.at[pl.ds(0, NX - 1)]
    pltpu.make_async_copy(sent, sent, send_sem.at[4]).wait()
    out.wait()


def per_device(incident, onset, beta, inverse_block, delay_blocks, history_sum):
    anywhere = pl.BlockSpec(memory_space=pl.ANY)
    dma = pltpu.SemaphoreType.DMA
    return pl.pallas_call(
        kernel,
        out_shape=(
            jax.ShapeDtypeStruct((STEPS, 64, 256), BF16),
            jax.ShapeDtypeStruct((1, 64, 128), F32),
        ),
        in_specs=[anywhere, pl.BlockSpec(memory_space=pltpu.SMEM), anywhere, anywhere, anywhere, anywhere],
        out_specs=(anywhere, anywhere),
        scratch_shapes=[
            pltpu.VMEM((64, 128), BF16),
            pltpu.VMEM((4096, 128), BF16),
            pltpu.VMEM((512, 512), BF16),
            pltpu.VMEM((2, 512, 512), BF16),
            pltpu.VMEM((2, 256, 128), BF16),
            pltpu.VMEM((NC, 1, 256), F32),
            pltpu.VMEM((STEPS, ROWS, 128), F32),
            pltpu.VMEM((NX, STEPS, ROWS, 128), F32),
            pltpu.VMEM((STEPS, NZ, ROWS, 512), F32),
            pltpu.VMEM((STEPS, NQ, ROWS, 512), F32),
            pltpu.VMEM((STEPS, NY * NQ * 16, 256), BF16),
            pltpu.VMEM((STEPS, 64, 128), F32),
            pltpu.VMEM((STEPS, 64, 128), F32),
            pltpu.VMEM((STEPS, 64, 256), BF16),
            dma((4,)),
            dma((7,)),
            dma((10,)),
            dma((STEPS,)),
            dma((STEPS,)),
            dma((STEPS,)),
            dma((STEPS,)),
            dma((STEPS,)),
            dma((STEPS,)),
            dma((STEPS,)),
            dma((STEPS,)),
            dma((STEPS + 1,)),
        ],
        compiler_params=pltpu.CompilerParams(
            collective_id=0, has_side_effects=True, vmem_limit_bytes=24 * 2**20
        ),
    )(incident, onset, beta.reshape(1, 256), inverse_block, delay_blocks, history_sum)


def solution(mesh):
    placed = (
        P(None, "row"),
        P(),
        P("delay"),
        P("row", "delay"),
        P("delay", None, "row"),
        P("delay", None, "row"),
    )
    return jax.shard_map(
        per_device,
        mesh=mesh,
        in_specs=placed,
        out_specs=(P(None, None, "delay"), P("delay", None, "row")),
        check_vma=False,
    )
```

time: 200 us -> 107 us (0.54)
  blocking collectives: 153 us -> 0 us
  Pallas kernels: 0 us -> 99.9 us
  starting transfers between devices: 21.8 us -> 0 us
  waiting for transfers between devices: 15.7 us -> 0 us
  other arithmetic: 3.13 us -> 0 us
  local copies, waits for them, and re-layouts: 2.87 us -> 5.46 us
    all_gather x6 -> x0, blocking collectives: 110 us -> none  [the longest x3 56.4 us: per_device(): gathered = lax.all_gather(own_block, 'delay', axis=1, tiled=True)]
    pallas_call x0 -> x1, Pallas kernels: none -> 99.9 us  [per_device(): pl.pallas_call(kernel, out_shape=(jax.ShapeDtypeStruct((STEPS, 64, 256),...]
    all_to_all x3 -> x0, blocking collectives: 43.3 us -> none  [sent_and_summed(): lax.all_to_all(in_blocks(value, dim, devices), axis, 0, 0, tiled=True)]
    all_to_all x3 -> x0, waiting for transfers between devices: 15.7 us -> none  [copy_for_each(): return lax.all_to_all(copies, axis, split_axis=0, concat_axis=0, tiled=True)]
    all_to_all x3 -> x0, starting transfers between devices: 11.7 us -> none  [copy_for_each(): return lax.all_to_all(copies, axis, split_axis=0, concat_axis=0, tiled=True)]
    ppermute x3 -> x0, starting transfers between devices: 10.1 us -> none  [passed_along(): return lax.ppermute(value, axis, pairs)]
    unnamed x10 -> x14, local copies, waits for them, and re-layouts: 0.66 us -> 5.46 us
  transfers between devices with their start and end apart: 6 -> 0, of which waited for: 3 -> 0; matrix products, arithmetic and copies ran while one was open for 1% -> 0% of each run, Pallas kernels for 0% -> 0%
where the time goes in v1:
time: 107 us; the launch traced here: 106 us
  Pallas kernels  99.9 us (93%)
  local copies, waits for them, and re-layouts  5.46 us (5%)
    pallas_call x1, Pallas kernels, per_device(): pl.pallas_call(kernel, out_shape=(jax.ShapeDtypeStruct((STEPS, 64, 256),...  99.9 us
    unnamed x14, local copies, waits for them, and re-layouts  5.46 us

profile of v1, /device:TPU:1, one launch (start us, length us, event | category | flops | bytes accessed | tf_op | source)
XLA Modules:
  0.0 106.1 jit_solution(7513518703032565305)
XLA Ops:
  0.6 0.0 copy-start.4
  0.6 0.0 copy-start.5
  0.7 0.7 copy-done.4
  1.3 0.0 copy-done.5
  1.3 0.0 copy-start
  1.3 1.2 %copy-done = bf16[1,4096,128]{2,1,0:T(8,128)(2,1)S(1)} copy-done((bf16[1,4096,128]{2,1,0:T(8,128)(2,1)S(1)}, bf16[1,4096,128]{2,1,0:T(8,128)(2,1)}, u32[]{:S(2)}) %copy-start) | copy-done | bytes 1048600
  2.5 0.0 copy-start.1
  2.5 0.8 copy-done.1
  3.4 0.0 copy-start.2
  3.4 0.8 copy-done.2
  4.1 0.0 copy-start.3
  4.1 0.7 copy-done.3
  4.9 99.9 %shard_map.77 = (bf16[3,64,256]{2,1,0:T(8,128)(2,1)S(1)}, f32[1,64,128]{2,1,0:T(8,128)S(1)}) custom-call(bf16[64,128]{1,0:T(8,128)(2,1)S(1)} %copy-done.3, s32[64]{0:T(128)S(1)} %copy-done.5, f32[1,256]{1,0:T(1,128)S(1)} %bitcast.1, bf16[128,256]{1,0:T(8,128)(2,1)S(1)} %copy-done.1, bf16[1,4096,128]{2,1,0:T(8,128)(2,1)S(1)} %copy-done, ...), custom_call_target="tpu_custom_call" | custom-call | tf_op jit(solution)/shard_map/pallas_call | solution.py:289
  104.8 0.6 copy.10
  105.4 0.6 copy.11
Async XLA Ops:
  0.6 0.7 copy-start.4
  0.6 0.7 copy-start.5
  1.3 1.2 %copy-start = (bf16[1,4096,128]{2,1,0:T(8,128)(2,1)S(1)}, bf16[1,4096,128]{2,1,0:T(8,128)(2,1)}, u32[]{:S(2)}) copy-start(bf16[1,4096,128]{2,1,0:T(8,128)(2,1)} %matrix.1) | copy-start | bytes 3145732
  2.5 0.8 copy-start.1
  3.4 0.8 copy-start.2
  4.1 0.7 copy-start.3

commit v2 on v0

v2 whole, which is shorter than its diff:
```python
import jax
import jax.numpy as jnp
from jax import lax
from jax.experimental import pallas as pl
from jax.experimental.pallas import tpu as pltpu
from jax.sharding import PartitionSpec as P

STEPS = 3
MESH = pl.DeviceIdType.MESH
F32, BF16 = jnp.float32, jnp.bfloat16
NY, NC, NZ, NX = 8, 2, 8, 4
ND = NY * NC
ROWS = 16


def far_first(n):
    return sorted(range(n), key=lambda i: -min(i, n - i))


LINE = [i for i in far_first(NZ) if i]
SLAB = [(dy, dc, dx) for dy in far_first(NY) for dx in far_first(NX) for dc in range(NC) if (dy, dc, dx) != (0, 0, 0)]
SLAB.sort(key=lambda o: -min(o[0], NY - o[0]) - min(o[2], NX - o[2]))
CORE = [o for o in SLAB if o[1] == 0]
DELAY = [o for o in SLAB if o[2] == 0]
OTHER_X = [i for i in far_first(NX) if i]


def kernel(
    incident, onset, beta, inverse, matrix, history,
    currents, carried,
    inc_v, hist_v, mat_v, inv_v, dl_v, stage_v, beta_v, first_v, res_v, base_v, zbuf, pre_v, xbuf, c_own, c_all,
    passed, future, first_src,
    load_sem, send_sem, recv_sem, z_send, z_recv, h_send, h_recv, x_send, x_recv, c_send, c_recv, m_send, m_recv,
    p_send, p_recv,
):
    d, r = lax.axis_index("delay"), lax.axis_index("row")
    y, c = d // NC, d % NC
    z, x = r // NX, r % NX

    def at(dy=0, dc=0, dz=0, dx=0):
        ty = lax.rem(y + dy, NY) if dy else y
        tc = 1 - c if dc else c
        tz = lax.rem(z + dz, NZ) if dz else z
        tx = lax.rem(x + dx, NX) if dx else x
        return (ty * NC + tc, tz * NX + tx)

    def remote(src, dst, send, recv, target):
        return pltpu.make_async_remote_copy(
            src_ref=src, dst_ref=dst, send_sem=send, recv_sem=recv, device_id=target, device_id_type=MESH
        )

    def arrived(ref, sem):
        pltpu.make_async_copy(ref, ref, sem).wait()

    left = arrived

    def rows_of(tx):
        return pl.ds(pl.multiple_of(tx * ROWS, ROWS), ROWS)

    own_rows = rows_of(x)

    loads = [
        pltpu.make_async_copy(src, dst, load_sem.at[i])
        for i, (src, dst) in enumerate(
            ((incident, inc_v), (history.at[0], hist_v), (beta, beta_v), (matrix.at[0], mat_v))
        )
    ]
    for load in loads:
        load.start()

    barrier = pltpu.get_barrier_semaphore()
    for i in LINE:
        pl.semaphore_signal(barrier, inc=1, device_id=at(dz=i), device_id_type=MESH)
    for dy, dc, dx in SLAB:
        pl.semaphore_signal(barrier, inc=1, device_id=at(dy, dc, 0, dx), device_id_type=MESH)

    for load in loads[:3]:
        load.wait()

    @pl.when(d < STEPS)
    def _():
        row_of = lax.broadcasted_iota(jnp.int32, (8, 128), 0)
        start = []
        for i in range(0, 64, 8):
            group = jnp.zeros((8, 128), jnp.int32)
            for e in range(8):
                group = jnp.where(row_of == e, onset[i + e], group)
            start.append(group)
        offset = (d - jnp.concatenate(start, axis=0)).astype(F32)
        envelope = jnp.where(offset >= 0.0, jnp.exp(-((offset - 1.0) ** 2) / 4.0), 0.0)
        res_v[...] = inc_v[...].astype(F32) * envelope - hist_v[...]
        first_src[...] = res_v[...].astype(BF16)

    pl.semaphore_wait(barrier, len(LINE) + len(SLAB))


    def cut(k):
        for dy, dc, dx in DELAY:
            t, tr = at(dy, dc)
            rows = pl.ds(pl.multiple_of(t * 256, 256), 256)
            remote(matrix.at[0, rows], stage_v.at[k], send_sem.at[1], recv_sem.at[1 + k], (t, tr)).start()
        pltpu.make_async_copy(matrix.at[0, pl.ds(k * 256, 256)], stage_v.at[k], recv_sem.at[1 + k]).start()

    def forward(k):
        arrived(stage_v.at[k], recv_sem.at[1 + k])
        columns = pl.ds(pl.multiple_of(x * 128, 128), 128)
        for i in OTHER_X:
            remote(stage_v.at[k], dl_v.at[k, :, columns], send_sem.at[4], recv_sem.at[3 + k], at(dx=i)).start()
        pltpu.make_async_copy(stage_v.at[k], dl_v.at[k, :, columns], recv_sem.at[3 + k]).start()

    @pl.when(d == 0)
    def _():
        for dy, dc, dx in SLAB:
            t = at(dy, dc, 0, dx)
            rows = rows_of(lax.rem(x + dx, NX)) if dx else own_rows
            remote(first_src.at[rows], first_v.at[x], send_sem.at[0], recv_sem.at[0], t).start()
        pltpu.make_async_copy(first_src.at[own_rows], first_v.at[x], recv_sem.at[0]).start()
        cut(0)

    inv_rows = pl.ds(pl.multiple_of(x * 128, 128), 128)
    for i in OTHER_X:
        remote(inverse, inv_v.at[inv_rows], send_sem.at[2], recv_sem.at[5], at(dx=i)).start()
    pltpu.make_async_copy(inverse, inv_v.at[inv_rows], recv_sem.at[5]).start()

    @pl.when(jnp.logical_and(d > 0, d < STEPS))
    def _():
        base_v[x] = res_v[own_rows]
        for i in OTHER_X:
            rows = rows_of(lax.rem(x + i, NX))
            remote(res_v.at[rows], base_v.at[x], send_sem.at[3], recv_sem.at[6], at(dx=i)).start()

    def pass_on(src, k):
        @pl.when(d > 0)
        def _():
            remote(src, passed.at[k], p_send.at[k], p_recv.at[k], (jnp.maximum(d - 1, 0), r)).start()

    def take(k):
        @pl.when(d < ND - 1)
        def _():
            arrived(passed.at[k], p_recv.at[k])

        return jnp.where(d < ND - 1, passed[k], 0.0)

    def share(s):
        arrived(c_all.at[s, c], c_recv.at[s])
        remote(c_all.at[s, c], c_all.at[s, c], m_send.at[s], m_recv.at[s], at(dc=1)).start()
        currents[s] = c_all[s, c, :, own_columns]

    own_columns = pl.ds(pl.multiple_of(y * 256, 256), 256)

    def product(s):
        total = jnp.zeros((64, 128), F32)
        for core in (c, 1 - c):
            if core is not c:
                arrived(c_all.at[s, core], m_recv.at[s])
            values = c_all[s, core]
            for i in range(NY):
                rows = pl.ds(pl.multiple_of((NC * i + core) * 256, 256), 256)
                total += jnp.dot(values[:, i * 256 : (i + 1) * 256], mat_v[rows], preferred_element_type=F32)
        return total

    def side_by_side(blocks):
        return jnp.concatenate([blocks[i].astype(F32) for i in range(NX)], axis=1)

    arrived(first_v, recv_sem.at[0])
    residual = side_by_side(first_v)
    for s in range(STEPS):
        if s == 0:
            arrived(inv_v, recv_sem.at[5])
        zbuf[s, z] = jnp.dot(residual.astype(BF16), inv_v[...], preferred_element_type=F32).astype(BF16)
        for i in LINE:
            remote(zbuf.at[s, z], zbuf.at[s, z], z_send.at[s], z_recv.at[s], at(dz=i)).start()
        if s == 0:
            pl.when(d == 1)(lambda: cut(1))
            forward(0)
            pass_on(history.at[0], 0)

            @pl.when(jnp.logical_and(d > 0, d < STEPS))
            def _():
                arrived(base_v.at[pl.ds(0, NX - 1)], recv_sem.at[6])

        if s == 2:
            share(0)
            loads[3].wait()
            future[0] = product(0) + take(0)
            pass_on(future.at[0], 1)

        arrived(zbuf.at[s, pl.ds(0, NZ - 1)], z_recv.at[s])
        solved = zbuf[s, 0].astype(F32)
        for i in range(1, NZ):
            solved += zbuf[s, i].astype(F32)
        current = (solved / (1.0 + beta_v[...] * solved * solved)).astype(BF16)
        c_own[s] = current
        if s < STEPS - 1:
            arrived(dl_v.at[s], recv_sem.at[3 + s])
            part = -jnp.dot(current, dl_v[0], preferred_element_type=F32)
            if s == 1:
                part -= jnp.dot(c_own[0], dl_v[1], preferred_element_type=F32)
            part += jnp.where(d == s + 1, side_by_side(base_v), 0.0)
            low, high = part[:, :256], part[:, 256:]
            pre_v[s, 0] = jnp.where(c == 0, high, low)
            remote(pre_v.at[s, 0], pre_v.at[s, 1], h_send.at[s], h_recv.at[s], at(dc=1)).start()
            arrived(pre_v.at[s, 1], h_recv.at[s])
            xbuf[s, c, y] = (jnp.where(c == 0, low, high) + pre_v[s, 1]).astype(BF16)
            for dy, dc, dx in DELAY:
                remote(xbuf.at[s, c, y], xbuf.at[s, c, y], x_send.at[s], x_recv.at[s], at(dy, dc)).start()

        landing = c_all.at[s, c, own_rows, own_columns]
        for dy, dc, dx in CORE:
            remote(c_own.at[s], landing, c_send.at[s], c_recv.at[s], at(dy, 0, 0, dx)).start()
        pltpu.make_async_copy(c_own.at[s], landing, c_recv.at[s]).start()
        if s < STEPS - 1:
            if s == 0:
                forward(1)
            arrived(mat_v.at[pl.ds(0, (ND - 1) * 32)], x_recv.at[s])
            halves = []
            for half in range(NC):
                total = xbuf[s, half, 0].astype(F32)
                for i in range(1, NY):
                    total += xbuf[s, half, i].astype(F32)
                halves.append(total)
            residual = jnp.concatenate(halves, axis=1)

    share(1)
    future[1] = product(1)
    future[1] = future[1] + take(1)
    pass_on(future.at[1], 2)

    for s in range(STEPS):
        left(zbuf.at[s, pl.ds(0, NZ - 1)], z_send.at[s])
        if s < STEPS - 1:
            left(pre_v.at[s, 0], h_send.at[s])
            left(mat_v.at[pl.ds(0, (ND - 1) * 32)], x_send.at[s])
            left(mat_v.at[pl.ds(0, (NY * NX - 1) * 32)], c_send.at[s])
            left(c_all.at[s, c], m_send.at[s])

        @pl.when(d > 0)
        def _(s=s):
            left(passed.at[s], p_send.at[s])

    left(inv_v.at[pl.ds(0, (NX - 1) * 128)], send_sem.at[2])
    left(mat_v.at[pl.ds(0, 2 * (NX - 1) * 256)], send_sem.at[4])

    @pl.when(d == 0)
    def _():
        left(mat_v.at[pl.ds(0, len(SLAB) * 16)], send_sem.at[0])

    @pl.when(d < 2)
    def _():
        left(mat_v.at[pl.ds(0, (ND - 1) * 256)], send_sem.at[1])

    @pl.when(jnp.logical_and(d > 0, d < STEPS))
    def _():
        left(base_v.at[pl.ds(0, NX - 1)], send_sem.at[3])

    share(2)
    carried[0] = product(2) + take(2)
    left(mat_v.at[pl.ds(0, (NY * NX - 1) * 32)], c_send.at[STEPS - 1])
    left(c_all.at[STEPS - 1, c], m_send.at[STEPS - 1])


def per_device(incident, onset, beta, inverse_block, delay_blocks, history_sum):
    hbm = pl.BlockSpec(memory_space=pltpu.HBM)
    vmem = pl.BlockSpec(memory_space=pltpu.VMEM)
    dma = pltpu.SemaphoreType.DMA
    steps = dma((STEPS,))
    return pl.pallas_call(
        kernel,
        out_shape=(
            pltpu.VMEM((STEPS, 64, 256), BF16),
            pltpu.VMEM((1, 64, 128), F32),
        ),
        in_specs=[hbm, pl.BlockSpec(memory_space=pltpu.SMEM), hbm, hbm, hbm, hbm],
        out_specs=(vmem, vmem),
        scratch_shapes=[
            pltpu.VMEM((64, 128), BF16),
            pltpu.VMEM((64, 128), F32),
            pltpu.VMEM((4096, 128), BF16),
            pltpu.VMEM((512, 256), BF16),
            pltpu.VMEM((2, 256, 512), BF16),
            pltpu.VMEM((2, 256, 128), BF16),
            pltpu.VMEM((1, 256), F32),
            pltpu.VMEM((NX, ROWS, 128), BF16),
            pltpu.VMEM((64, 128), F32),
            pltpu.VMEM((NX, ROWS, 128), F32),
            pltpu.VMEM((STEPS, NZ, ROWS, 256), BF16),
            pltpu.VMEM((STEPS - 1, 2, ROWS, 256), F32),
            pltpu.VMEM((STEPS - 1, NC, NY, ROWS, 256), BF16),
            pltpu.VMEM((STEPS, ROWS, 256), BF16),
            pltpu.VMEM((STEPS, NC, 64, 2048), BF16),
            pltpu.VMEM((STEPS, 64, 128), F32),
            pltpu.VMEM((STEPS - 1, 64, 128), F32),
            pltpu.VMEM((64, 128), BF16),
            dma((4,)),
            dma((5,)),
            dma((7,)),
            *[steps] * 12,
        ],
        compiler_params=pltpu.CompilerParams(
            collective_id=0, has_side_effects=True, vmem_limit_bytes=60 * 10**6
        ),
    )(incident, onset, beta.reshape(1, 256), inverse_block, delay_blocks, history_sum)


def solution(mesh):
    placed = (
        P(None, "row"),
        P(),
        P("delay"),
        P("row", "delay"),
        P("delay", None, "row"),
        P("delay", None, "row"),
    )
    return jax.shard_map(
        per_device,
        mesh=mesh,
        in_specs=placed,
        out_specs=(P(None, None, "delay"), P("delay", None, "row")),
        check_vma=False,
    )
```

time: 200 us -> 69.8 us (0.35)
  blocking collectives: 153 us -> 0 us
  Pallas kernels: 0 us -> 67.7 us
  starting transfers between devices: 21.8 us -> 0 us
  waiting for transfers between devices: 15.7 us -> 0 us
  other arithmetic: 3.13 us -> 0 us
    all_gather x6 -> x0, blocking collectives: 110 us -> none  [the longest x3 56.4 us: per_device(): gathered = lax.all_gather(own_block, 'delay', axis=1, tiled=True)]
    pallas_call x0 -> x1, Pallas kernels: none -> 67.7 us  [per_device(): pl.pallas_call(kernel, out_shape=(pltpu.VMEM((STEPS, 64, 256), BF16), plt...]
    all_to_all x3 -> x0, blocking collectives: 43.3 us -> none  [sent_and_summed(): lax.all_to_all(in_blocks(value, dim, devices), axis, 0, 0, tiled=True)]
    all_to_all x3 -> x0, waiting for transfers between devices: 15.7 us -> none  [copy_for_each(): return lax.all_to_all(copies, axis, split_axis=0, concat_axis=0, tiled=True)]
    all_to_all x3 -> x0, starting transfers between devices: 11.7 us -> none  [copy_for_each(): return lax.all_to_all(copies, axis, split_axis=0, concat_axis=0, tiled=True)]
    ppermute x3 -> x0, starting transfers between devices: 10.1 us -> none  [passed_along(): return lax.ppermute(value, axis, pairs)]
  transfers between devices with their start and end apart: 6 -> 0, of which waited for: 3 -> 0; matrix products, arithmetic and copies ran while one was open for 1% -> 0% of each run, Pallas kernels for 0% -> 0%
where the time goes in v2:
time: 69.8 us; the launch traced here: 69.6 us
  Pallas kernels  67.7 us (97%)
  local copies, waits for them, and re-layouts  1.26 us (2%)
    pallas_call x1, Pallas kernels, per_device(): pl.pallas_call(kernel, out_shape=(pltpu.VMEM((STEPS, 64, 256), BF16), plt...  67.7 us

profile of v2, /device:TPU:1, one launch (start us, length us, event | category | flops | bytes accessed | tf_op | source)
XLA Modules:
  0.0 69.6 jit_solution(17104767639527166452)
XLA Ops:
  0.6 67.7 %shard_map.77 = (bf16[3,64,256]{2,1,0:T(8,128)(2,1)S(1)}, f32[1,64,128]{2,1,0:T(8,128)S(1)}) custom-call(bf16[64,128]{1,0:T(8,128)(2,1)} %incident.1, s32[64]{0:T(128)} %onset.1, f32[1,256]{1,0:T(1,128)} %bitcast.1, bf16[128,256]{1,0:T(8,128)(2,1)} %inverse.1, bf16[1,4096,128]{2,1,0:T(8,128)(2,1)} %matrix.1, f32[1,64,128]{2,1,0:T(8,128)} %history.1), custom_call_target="tpu_custom_call" | custom-call | tf_op jit(solution)/shard_map/pallas_call | solution.py:267
  68.3 0.6 copy.10
  69.0 0.6 copy.11

commit v3 on v2

--- a/solution.py
+++ b/solution.py
@@ -28,7 +28,7 @@
 def kernel(
     incident, onset, beta, inverse, matrix, history,
     currents, carried,
-    inc_v, hist_v, mat_v, inv_v, dl_v, stage_v, beta_v, first_v, res_v, base_v, zbuf, pre_v, xbuf, c_own, c_all,
+    onset_v, inc_v, hist_v, mat_v, inv_v, dl_v, stage_v, beta_v, first_v, res_v, base_v, zbuf, pre_v, xbuf, c_own, c_all,
     passed, future, first_src,
     load_sem, send_sem, recv_sem, z_send, z_recv, h_send, h_recv, x_send, x_recv, c_send, c_recv, m_send, m_recv,
     p_send, p_recv,
@@ -62,7 +62,7 @@
     loads = [
         pltpu.make_async_copy(src, dst, load_sem.at[i])
         for i, (src, dst) in enumerate(
-            ((incident, inc_v), (history.at[0], hist_v), (beta, beta_v), (matrix.at[0], mat_v))
+            ((onset, onset_v), (incident, inc_v), (history.at[0], hist_v), (beta, beta_v), (matrix.at[0], mat_v))
         )
     ]
     for load in loads:
@@ -74,7 +74,7 @@
     for dy, dc, dx in SLAB:
         pl.semaphore_signal(barrier, inc=1, device_id=at(dy, dc, 0, dx), device_id_type=MESH)
 
-    for load in loads[:3]:
+    for load in loads[:4]:
         load.wait()
 
     @pl.when(d < STEPS)
@@ -84,7 +84,7 @@
         for i in range(0, 64, 8):
             group = jnp.zeros((8, 128), jnp.int32)
             for e in range(8):
-                group = jnp.where(row_of == e, onset[i + e], group)
+                group = jnp.where(row_of == e, onset_v[i + e], group)
             start.append(group)
         offset = (d - jnp.concatenate(start, axis=0)).astype(F32)
         envelope = jnp.where(offset >= 0.0, jnp.exp(-((offset - 1.0) ** 2) / 4.0), 0.0)
@@ -94,19 +94,21 @@
     pl.semaphore_wait(barrier, len(LINE) + len(SLAB))
 
 
-    def cut(k):
+    def cut(k, half):
         for dy, dc, dx in DELAY:
             t, tr = at(dy, dc)
-            rows = pl.ds(pl.multiple_of(t * 256, 256), 256)
-            remote(matrix.at[0, rows], stage_v.at[k], send_sem.at[1], recv_sem.at[1 + k], (t, tr)).start()
-        pltpu.make_async_copy(matrix.at[0, pl.ds(k * 256, 256)], stage_v.at[k], recv_sem.at[1 + k]).start()
-
-    def forward(k):
-        arrived(stage_v.at[k], recv_sem.at[1 + k])
-        columns = pl.ds(pl.multiple_of(x * 128, 128), 128)
+            rows = pl.ds(pl.multiple_of(t * 256 + half * 128, 128), 128)
+            sems = send_sem.at[1], recv_sem.at[1 + 2 * k + half]
+            remote(matrix.at[0, rows], stage_v.at[k, half], *sems, (t, tr)).start()
+        rows = pl.ds(k * 256 + half * 128, 128)
+        pltpu.make_async_copy(matrix.at[0, rows], stage_v.at[k, half], recv_sem.at[1 + 2 * k + half]).start()
+
+    def forward(k, half):
+        arrived(stage_v.at[k, half], recv_sem.at[1 + 2 * k + half])
+        part = (pl.ds(half * 128, 128), pl.ds(pl.multiple_of(x * 128, 128), 128))
         for i in OTHER_X:
-            remote(stage_v.at[k], dl_v.at[k, :, columns], send_sem.at[4], recv_sem.at[3 + k], at(dx=i)).start()
-        pltpu.make_async_copy(stage_v.at[k], dl_v.at[k, :, columns], recv_sem.at[3 + k]).start()
+            remote(stage_v.at[k, half], dl_v.at[(k,) + part], send_sem.at[4], recv_sem.at[7 + k], at(dx=i)).start()
+        pltpu.make_async_copy(stage_v.at[k, half], dl_v.at[(k,) + part], recv_sem.at[7 + k]).start()
 
     @pl.when(d == 0)
     def _():
@@ -115,7 +117,8 @@
             rows = rows_of(lax.rem(x + dx, NX)) if dx else own_rows
             remote(first_src.at[rows], first_v.at[x], send_sem.at[0], recv_sem.at[0], t).start()
         pltpu.make_async_copy(first_src.at[own_rows], first_v.at[x], recv_sem.at[0]).start()
-        cut(0)
+        cut(0, 0)
+        cut(0, 1)
 
     inv_rows = pl.ds(pl.multiple_of(x * 128, 128), 128)
     for i in OTHER_X:
@@ -147,6 +150,12 @@
         currents[s] = c_all[s, c, :, own_columns]
 
     own_columns = pl.ds(pl.multiple_of(y * 256, 256), 256)
+
+    def send_values(s):
+        landing = c_all.at[s, c, own_rows, own_columns]
+        for dy, dc, dx in CORE:
+            remote(c_own.at[s], landing, c_send.at[s], c_recv.at[s], at(dy, 0, 0, dx)).start()
+        pltpu.make_async_copy(c_own.at[s], landing, c_recv.at[s]).start()
 
     def product(s):
         total = jnp.zeros((64, 128), F32)
@@ -171,17 +180,25 @@
         for i in LINE:
             remote(zbuf.at[s, z], zbuf.at[s, z], z_send.at[s], z_recv.at[s], at(dz=i)).start()
         if s == 0:
-            pl.when(d == 1)(lambda: cut(1))
-            forward(0)
+
+            @pl.when(d == 1)
+            def _():
+                cut(1, 0)
+                cut(1, 1)
+
+            forward(0, 0)
+            forward(0, 1)
             pass_on(history.at[0], 0)
 
             @pl.when(jnp.logical_and(d > 0, d < STEPS))
             def _():
                 arrived(base_v.at[pl.ds(0, NX - 1)], recv_sem.at[6])
 
+        if s == 1:
+            send_values(0)
         if s == 2:
             share(0)
-            loads[3].wait()
+            loads[4].wait()
             future[0] = product(0) + take(0)
             pass_on(future.at[0], 1)
 
@@ -192,7 +209,7 @@
         current = (solved / (1.0 + beta_v[...] * solved * solved)).astype(BF16)
         c_own[s] = current
         if s < STEPS - 1:
-            arrived(dl_v.at[s], recv_sem.at[3 + s])
+            arrived(dl_v.at[s], recv_sem.at[7 + s])
             part = -jnp.dot(current, dl_v[0], preferred_element_type=F32)
             if s == 1:
                 part -= jnp.dot(c_own[0], dl_v[1], preferred_element_type=F32)
@@ -205,13 +222,12 @@
             for dy, dc, dx in DELAY:
                 remote(xbuf.at[s, c, y], xbuf.at[s, c, y], x_send.at[s], x_recv.at[s], at(dy, dc)).start()
 
-        landing = c_all.at[s, c, own_rows, own_columns]
-        for dy, dc, dx in CORE:
-            remote(c_own.at[s], landing, c_send.at[s], c_recv.at[s], at(dy, 0, 0, dx)).start()
-        pltpu.make_async_copy(c_own.at[s], landing, c_recv.at[s]).start()
+        if s > 0:
+            send_values(s)
         if s < STEPS - 1:
             if s == 0:
-                forward(1)
+                forward(1, 0)
+                forward(1, 1)
             arrived(mat_v.at[pl.ds(0, (ND - 1) * 32)], x_recv.at[s])
             halves = []
             for half in range(NC):
@@ -254,8 +270,8 @@
         left(base_v.at[pl.ds(0, NX - 1)], send_sem.at[3])
 
     share(2)
+    left(mat_v.at[pl.ds(0, (NY * NX - 1) * 32)], c_send.at[STEPS - 1])
     carried[0] = product(2) + take(2)
-    left(mat_v.at[pl.ds(0, (NY * NX - 1) * 32)], c_send.at[STEPS - 1])
     left(c_all.at[STEPS - 1, c], m_send.at[STEPS - 1])
 
 
@@ -270,15 +286,16 @@
             pltpu.VMEM((STEPS, 64, 256), BF16),
             pltpu.VMEM((1, 64, 128), F32),
         ),
-        in_specs=[hbm, pl.BlockSpec(memory_space=pltpu.SMEM), hbm, hbm, hbm, hbm],
+        in_specs=[hbm] * 6,
         out_specs=(vmem, vmem),
         scratch_shapes=[
+            pltpu.SMEM((64,), jnp.int32),
             pltpu.VMEM((64, 128), BF16),
             pltpu.VMEM((64, 128), F32),
             pltpu.VMEM((4096, 128), BF16),
             pltpu.VMEM((512, 256), BF16),
             pltpu.VMEM((2, 256, 512), BF16),
-            pltpu.VMEM((2, 256, 128), BF16),
+            pltpu.VMEM((2, 2, 128, 128), BF16),
             pltpu.VMEM((1, 256), F32),
             pltpu.VMEM((NX, ROWS, 128), BF16),
             pltpu.VMEM((64, 128), F32),
@@ -291,9 +308,9 @@
             pltpu.VMEM((STEPS, 64, 128), F32),
             pltpu.VMEM((STEPS - 1, 64, 128), F32),
             pltpu.VMEM((64, 128), BF16),
-            dma((4,)),
             dma((5,)),
-            dma((7,)),
+            dma((5,)),
+            dma((11,)),
             *[steps] * 12,
         ],
         compiler_params=pltpu.CompilerParams(

time: 69.8 us -> 67.3 us (0.964)
  Pallas kernels: 67.7 us -> 65.2 us
    pallas_call x1, Pallas kernels: 67.7 us -> 65.2 us  [per_device(): pl.pallas_call(kernel, out_shape=(pltpu.VMEM((STEPS, 64, 256), BF16), plt...]
where the time goes in v3:
time: 67.3 us; the launch traced here: 67.1 us
  Pallas kernels  65.2 us (97%)
  local copies, waits for them, and re-layouts  1.26 us (2%)
    pallas_call x1, Pallas kernels, per_device(): pl.pallas_call(kernel, out_shape=(pltpu.VMEM((STEPS, 64, 256), BF16), plt...  65.2 us

profile of v3, /device:TPU:1, one launch (start us, length us, event | category | flops | bytes accessed | tf_op | source)
XLA Modules:
  0.0 67.1 jit_solution(11645816562288454724)
XLA Ops:
  0.6 65.2 %shard_map.77 = (bf16[3,64,256]{2,1,0:T(8,128)(2,1)S(1)}, f32[1,64,128]{2,1,0:T(8,128)S(1)}) custom-call(bf16[64,128]{1,0:T(8,128)(2,1)} %incident.1, s32[64]{0:T(128)} %onset.1, f32[1,256]{1,0:T(1,128)} %bitcast.1, bf16[128,256]{1,0:T(8,128)(2,1)} %inverse.1, bf16[1,4096,128]{2,1,0:T(8,128)(2,1)} %matrix.1, f32[1,64,128]{2,1,0:T(8,128)} %history.1), custom_call_target="tpu_custom_call" | custom-call | tf_op jit(solution)/shard_map/pallas_call | solution.py:283
  65.9 0.6 copy.10
  66.5 0.6 copy.11

commit v4 on v3

--- a/solution.py
+++ b/solution.py
@@ -21,6 +21,11 @@
 SLAB = [(dy, dc, dx) for dy in far_first(NY) for dx in far_first(NX) for dc in range(NC) if (dy, dc, dx) != (0, 0, 0)]
 SLAB.sort(key=lambda o: -min(o[0], NY - o[0]) - min(o[2], NX - o[2]))
 CORE = [o for o in SLAB if o[1] == 0]
+FAR = [o for o in CORE if min(o[0], NY - o[0]) > 1]
+NEAR = [o for o in CORE if o not in FAR]
+FAR_SLOTS, NEAR_SLOTS = (2, 5), ((0, 2), (7, 1))
+FAR_BLOCKS, NEAR_BLOCKS = 5 * NX, 3 * NX
+BLOCK = 32
 DELAY = [o for o in SLAB if o[2] == 0]
 OTHER_X = [i for i in far_first(NX) if i]
 
@@ -28,10 +33,10 @@
 def kernel(
     incident, onset, beta, inverse, matrix, history,
     currents, carried,
-    onset_v, inc_v, hist_v, mat_v, inv_v, dl_v, stage_v, beta_v, first_v, res_v, base_v, zbuf, pre_v, xbuf, c_own, c_all,
+    onset_v, inc_v, hist_v, mat_v, inv_v, dl_v, stage_v, beta_v, first_v, res_v, base_v, zbuf, pre_v, xbuf, halves, c_own, c_all,
     passed, future, first_src,
     load_sem, send_sem, recv_sem, z_send, z_recv, h_send, h_recv, x_send, x_recv, c_send, c_recv, m_send, m_recv,
-    p_send, p_recv,
+    p_send, p_recv, r_send, r_recv, next_sem,
 ):
     d, r = lax.axis_index("delay"), lax.axis_index("row")
     y, c = d // NC, d % NC
@@ -144,50 +149,68 @@
 
         return jnp.where(d < ND - 1, passed[k], 0.0)
 
-    def share(s):
-        arrived(c_all.at[s, c], c_recv.at[s])
-        remote(c_all.at[s, c], c_all.at[s, c], m_send.at[s], m_recv.at[s], at(dc=1)).start()
-        currents[s] = c_all[s, c, :, own_columns]
-
-    own_columns = pl.ds(pl.multiple_of(y * 256, 256), 256)
+    def columns_of(slot, slots=1):
+        return pl.ds(slot * 256, slots * 256)
 
     def send_values(s):
-        landing = c_all.at[s, c, own_rows, own_columns]
-        for dy, dc, dx in CORE:
-            remote(c_own.at[s], landing, c_send.at[s], c_recv.at[s], at(dy, 0, 0, dx)).start()
-        pltpu.make_async_copy(c_own.at[s], landing, c_recv.at[s]).start()
+        for part, where in enumerate((FAR, NEAR)):
+            for dy, dc, dx in where:
+                landing = c_all.at[s, c, own_rows, columns_of((NY - dy) % NY)]
+                remote(c_own.at[s], landing, c_send.at[s], c_recv.at[s, part], at(dy, 0, 0, dx)).start()
+        pltpu.make_async_copy(c_own.at[s], c_all.at[s, c, own_rows, columns_of(0)], c_recv.at[s, 1]).start()
+
+    def share(s, part):
+        arrived(mat_v.at[pl.ds(0, FAR_BLOCKS * BLOCK if part == 0 else NEAR_BLOCKS * BLOCK)], c_recv.at[s, part])
+        for columns in (FAR_SLOTS,) if part == 0 else NEAR_SLOTS:
+            half = c_all.at[s, c, :, columns_of(*columns)]
+            remote(half, half, m_send.at[s], m_recv.at[s, part], at(dc=1)).start()
+        if part == 1:
+            currents[s] = c_all[s, c, :, columns_of(0)]
+
+    def multiply(s, part, core):
+        total = jnp.zeros((64, 128), F32)
+        for first, slots in (FAR_SLOTS,) if part == 0 else NEAR_SLOTS:
+            for slot in range(first, first + slots):
+                rows = pl.ds(pl.multiple_of((NC * lax.rem(y + slot, NY) + core) * 256, 256), 256)
+                total += jnp.dot(c_all[s, core, :, columns_of(slot)], mat_v[rows], preferred_element_type=F32)
+        return total
 
     def product(s):
-        total = jnp.zeros((64, 128), F32)
-        for core in (c, 1 - c):
-            if core is not c:
-                arrived(c_all.at[s, core], m_recv.at[s])
-            values = c_all[s, core]
-            for i in range(NY):
-                rows = pl.ds(pl.multiple_of((NC * i + core) * 256, 256), 256)
-                total += jnp.dot(values[:, i * 256 : (i + 1) * 256], mat_v[rows], preferred_element_type=F32)
+        share(s, 0)
+        total = multiply(s, 0, c)
+        share(s, 1)
+        total += multiply(s, 1, c)
+        for part, blocks in enumerate((FAR_BLOCKS, NEAR_BLOCKS)):
+            arrived(mat_v.at[pl.ds(0, blocks * BLOCK)], m_recv.at[s, part])
+            total += multiply(s, part, 1 - c)
         return total
 
     def side_by_side(blocks):
         return jnp.concatenate([blocks[i].astype(F32) for i in range(NX)], axis=1)
 
     arrived(first_v, recv_sem.at[0])
-    residual = side_by_side(first_v)
+    residual = jnp.concatenate([first_v[i] for i in range(NX)], axis=1)
     for s in range(STEPS):
         if s == 0:
             arrived(inv_v, recv_sem.at[5])
-        zbuf[s, z] = jnp.dot(residual.astype(BF16), inv_v[...], preferred_element_type=F32).astype(BF16)
+        zbuf[s, z] = jnp.dot(residual, inv_v[...], preferred_element_type=F32).astype(BF16)
         for i in LINE:
             remote(zbuf.at[s, z], zbuf.at[s, z], z_send.at[s], z_recv.at[s], at(dz=i)).start()
         if s == 0:
+            forward(0, 0)
+            forward(0, 1)
+
+            @pl.when(d == 0)
+            def _():
+                left(mat_v.at[pl.ds(0, (ND - 1) * 256)], send_sem.at[1])
+                pl.semaphore_signal(next_sem, inc=1, device_id=at(dc=1), device_id_type=MESH)
 
             @pl.when(d == 1)
             def _():
+                pl.semaphore_wait(next_sem, 1)
                 cut(1, 0)
                 cut(1, 1)
 
-            forward(0, 0)
-            forward(0, 1)
             pass_on(history.at[0], 0)
 
             @pl.when(jnp.logical_and(d > 0, d < STEPS))
@@ -197,7 +220,6 @@
         if s == 1:
             send_values(0)
         if s == 2:
-            share(0)
             loads[4].wait()
             future[0] = product(0) + take(0)
             pass_on(future.at[0], 1)
@@ -218,9 +240,9 @@
             pre_v[s, 0] = jnp.where(c == 0, high, low)
             remote(pre_v.at[s, 0], pre_v.at[s, 1], h_send.at[s], h_recv.at[s], at(dc=1)).start()
             arrived(pre_v.at[s, 1], h_recv.at[s])
-            xbuf[s, c, y] = (jnp.where(c == 0, low, high) + pre_v[s, 1]).astype(BF16)
-            for dy, dc, dx in DELAY:
-                remote(xbuf.at[s, c, y], xbuf.at[s, c, y], x_send.at[s], x_recv.at[s], at(dy, dc)).start()
+            xbuf[s, y] = (jnp.where(c == 0, low, high) + pre_v[s, 1]).astype(BF16)
+            for i in LINE:
+                remote(xbuf.at[s, y], xbuf.at[s, y], x_send.at[s], x_recv.at[s], at(i)).start()
 
         if s > 0:
             send_values(s)
@@ -228,16 +250,15 @@
             if s == 0:
                 forward(1, 0)
                 forward(1, 1)
-            arrived(mat_v.at[pl.ds(0, (ND - 1) * 32)], x_recv.at[s])
-            halves = []
-            for half in range(NC):
-                total = xbuf[s, half, 0].astype(F32)
-                for i in range(1, NY):
-                    total += xbuf[s, half, i].astype(F32)
-                halves.append(total)
-            residual = jnp.concatenate(halves, axis=1)
-
-    share(1)
+            arrived(xbuf.at[s, pl.ds(0, NY - 1)], x_recv.at[s])
+            total = xbuf[s, 0].astype(F32)
+            for i in range(1, NY):
+                total += xbuf[s, i].astype(F32)
+            halves[s, c] = total.astype(BF16)
+            remote(halves.at[s, c], halves.at[s, c], r_send.at[s], r_recv.at[s], at(dc=1)).start()
+            arrived(halves.at[s, 1 - c], r_recv.at[s])
+            residual = jnp.concatenate([halves[s, 0], halves[s, 1]], axis=1)
+
     future[1] = product(1)
     future[1] = future[1] + take(1)
     pass_on(future.at[1], 2)
@@ -246,8 +267,9 @@
         left(zbuf.at[s, pl.ds(0, NZ - 1)], z_send.at[s])
         if s < STEPS - 1:
             left(pre_v.at[s, 0], h_send.at[s])
-            left(mat_v.at[pl.ds(0, (ND - 1) * 32)], x_send.at[s])
-            left(mat_v.at[pl.ds(0, (NY * NX - 1) * 32)], c_send.at[s])
+            left(xbuf.at[s, pl.ds(0, NY - 1)], x_send.at[s])
+            left(halves.at[s, c], r_send.at[s])
+            left(mat_v.at[pl.ds(0, len(CORE) * BLOCK)], c_send.at[s])
             left(c_all.at[s, c], m_send.at[s])
 
         @pl.when(d > 0)
@@ -261,7 +283,7 @@
     def _():
         left(mat_v.at[pl.ds(0, len(SLAB) * 16)], send_sem.at[0])
 
-    @pl.when(d < 2)
+    @pl.when(d == 1)
     def _():
         left(mat_v.at[pl.ds(0, (ND - 1) * 256)], send_sem.at[1])
 
@@ -269,9 +291,9 @@
     def _():
         left(base_v.at[pl.ds(0, NX - 1)], send_sem.at[3])
 
-    share(2)
-    left(mat_v.at[pl.ds(0, (NY * NX - 1) * 32)], c_send.at[STEPS - 1])
-    carried[0] = product(2) + take(2)
+    total = product(2)
+    carried[0] = total + take(2)
+    left(mat_v.at[pl.ds(0, len(CORE) * BLOCK)], c_send.at[STEPS - 1])
     left(c_all.at[STEPS - 1, c], m_send.at[STEPS - 1])
 
 
@@ -302,7 +324,8 @@
             pltpu.VMEM((NX, ROWS, 128), F32),
             pltpu.VMEM((STEPS, NZ, ROWS, 256), BF16),
             pltpu.VMEM((STEPS - 1, 2, ROWS, 256), F32),
-            pltpu.VMEM((STEPS - 1, NC, NY, ROWS, 256), BF16),
+            pltpu.VMEM((STEPS - 1, NY, ROWS, 256), BF16),
+            pltpu.VMEM((STEPS - 1, NC, ROWS, 256), BF16),
             pltpu.VMEM((STEPS, ROWS, 256), BF16),
             pltpu.VMEM((STEPS, NC, 64, 2048), BF16),
             pltpu.VMEM((STEPS, 64, 128), F32),
@@ -311,7 +334,12 @@
             dma((5,)),
             dma((5,)),
             dma((11,)),
-            *[steps] * 12,
+            *[steps] * 7,
+            dma((STEPS, 2)),
+            steps,
+            dma((STEPS, 2)),
+            *[steps] * 4,
+            pltpu.SemaphoreType.REGULAR,
         ],
         compiler_params=pltpu.CompilerParams(
             collective_id=0, has_side_effects=True, vmem_limit_bytes=60 * 10**6

time: 67.3 us -> 66.2 us (0.984)
  Pallas kernels: 65.2 us -> 64.2 us
    pallas_call x1, Pallas kernels: 65.2 us -> 64.2 us  [per_device(): pl.pallas_call(kernel, out_shape=(pltpu.VMEM((STEPS, 64, 256), BF16), plt...]
where the time goes in v4:
time: 66.2 us; the launch traced here: 66.1 us
  Pallas kernels  64.2 us (97%)
  local copies, waits for them, and re-layouts  1.26 us (2%)
    pallas_call x1, Pallas kernels, per_device(): pl.pallas_call(kernel, out_shape=(pltpu.VMEM((STEPS, 64, 256), BF16), plt...  64.2 us

profile of v4, /device:TPU:1, one launch (start us, length us, event | category | flops | bytes accessed | tf_op | source)
XLA Modules:
  0.0 66.1 jit_solution(3963712598675859358)
XLA Ops:
  0.6 64.2 %shard_map.77 = (bf16[3,64,256]{2,1,0:T(8,128)(2,1)S(1)}, f32[1,64,128]{2,1,0:T(8,128)S(1)}) custom-call(bf16[64,128]{1,0:T(8,128)(2,1)} %incident.1, s32[64]{0:T(128)} %onset.1, f32[1,256]{1,0:T(1,128)} %bitcast.1, bf16[128,256]{1,0:T(8,128)(2,1)} %inverse.1, bf16[1,4096,128]{2,1,0:T(8,128)(2,1)} %matrix.1, f32[1,64,128]{2,1,0:T(8,128)} %history.1), custom_call_target="tpu_custom_call" | custom-call | tf_op jit(solution)/shard_map/pallas_call | solution.py:305
  64.9 0.6 copy.10
  65.5 0.6 copy.11

commit v5 on v4

v5 whole, which is shorter than its diff:
```python
import jax
import jax.numpy as jnp
from jax import lax
from jax.experimental import pallas as pl
from jax.experimental.pallas import tpu as pltpu
from jax.sharding import PartitionSpec as P

STEPS = 3
MESH = pl.DeviceIdType.MESH
F32, BF16 = jnp.float32, jnp.bfloat16
NY, NC, NZ, NX = 8, 2, 8, 4
ND = NY * NC
ROWS = 8


def far_first(n):
    return sorted(range(n), key=lambda i: -min(i, n - i))


LINE = [i for i in far_first(NZ) if i]
SLAB = [(dy, dc, dx) for dy in far_first(NY) for dx in far_first(NX) for dc in range(NC) if (dy, dc, dx) != (0, 0, 0)]
SLAB.sort(key=lambda o: -min(o[0], NY - o[0]) - min(o[2], NX - o[2]))
CORE = [o for o in SLAB if o[1] == 0]
FAR = [o for o in CORE if min(o[0], NY - o[0]) > 1]
NEAR = [o for o in CORE if o not in FAR]
FAR_SLOTS, NEAR_SLOTS = (2, 5), ((0, 2), (7, 1))
FAR_BLOCKS, NEAR_BLOCKS = 5 * NX, 3 * NX
BLOCK = 32
DELAY = [o for o in SLAB if o[2] == 0]
OTHER_X = [i for i in far_first(NX) if i]


def kernel(
    incident, onset, beta, inverse, matrix, history,
    currents, carried,
    onset_v, inc_v, hist_v, mat_v, inv_v, dl_v, stage_v, beta_v, first_v, res_v, base_v, zbuf, xbuf, c_own, c_all,
    passed, future,
    load_sem, send_sem, recv_sem, t_send, t_recv, z_send, z_recv, x_send, x_recv, c_send, c_recv, m_send, m_recv,
    p_send, p_recv, next_sem,
):
    d, r = lax.axis_index("delay"), lax.axis_index("row")
    y, c = d // NC, d % NC
    z, x = r // NX, r % NX

    def at(dy=0, dc=0, dz=0, dx=0):
        ty = lax.rem(y + dy, NY) if dy else y
        tc = 1 - c if dc else c
        tz = lax.rem(z + dz, NZ) if dz else z
        tx = lax.rem(x + dx, NX) if dx else x
        return (ty * NC + tc, tz * NX + tx)

    def remote(src, dst, send, recv, target):
        return pltpu.make_async_remote_copy(
            src_ref=src, dst_ref=dst, send_sem=send, recv_sem=recv, device_id=target, device_id_type=MESH
        )

    def arrived(ref, sem):
        pltpu.make_async_copy(ref, ref, sem).wait()

    left = arrived

    def rows_of(dx, dc):
        t = (lax.rem(x + dx, NX) if dx else x) * NC + (1 - c if dc else c)
        return pl.ds(pl.multiple_of(t * ROWS, ROWS), ROWS)

    own_rows = rows_of(0, 0)

    def stacked(wide):
        return jnp.concatenate([wide[:, :256], wide[:, 256:]], axis=0)

    def unstacked(tall):
        return jnp.concatenate([tall[:ROWS], tall[ROWS:]], axis=1)

    def halves(block):
        block = block.astype(F32).reshape(NX, NC, ROWS, 256)
        return block[:, 0].reshape(NX * ROWS, 256), block[:, 1].reshape(NX * ROWS, 256)

    def in_order(zeroth, first, width):
        parts = [v.reshape(NX, 1, ROWS, width) for v in (zeroth, first)]
        return jnp.concatenate(parts, axis=1).reshape(64, width)

    loads = [
        pltpu.make_async_copy(src, dst, load_sem.at[i])
        for i, (src, dst) in enumerate(
            ((onset, onset_v), (incident, inc_v), (history.at[0], hist_v), (beta, beta_v.at[c]), (matrix.at[0], mat_v))
        )
    ]
    for load in loads:
        load.start()

    barrier = pltpu.get_barrier_semaphore()
    for i in LINE:
        pl.semaphore_signal(barrier, inc=1, device_id=at(dz=i), device_id_type=MESH)
    for dy, dc, dx in SLAB:
        pl.semaphore_signal(barrier, inc=1, device_id=at(dy, dc, 0, dx), device_id_type=MESH)

    for load in loads[:4]:
        load.wait()

    @pl.when(d < STEPS)
    def _():
        row_of = lax.broadcasted_iota(jnp.int32, (8, 128), 0)
        start = []
        for i in range(0, 64, 8):
            group = jnp.zeros((8, 128), jnp.int32)
            for e in range(8):
                group = jnp.where(row_of == e, onset_v[i + e], group)
            start.append(group)
        offset = (d - jnp.concatenate(start, axis=0)).astype(F32)
        envelope = jnp.where(offset >= 0.0, jnp.exp(-((offset - 1.0) ** 2) / 4.0), 0.0)
        res_v[...] = inc_v[...].astype(F32) * envelope - hist_v[...]

    pl.semaphore_wait(barrier, len(LINE) + len(SLAB))


    def cut(k, half):
        for dy, dc, dx in DELAY:
            t, tr = at(dy, dc)
            rows = pl.ds(pl.multiple_of(t * 256 + half * 128, 128), 128)
            sems = send_sem.at[1], recv_sem.at[1 + 2 * k + half]
            remote(matrix.at[0, rows], stage_v.at[k, half], *sems, (t, tr)).start()
        rows = pl.ds(k * 256 + half * 128, 128)
        pltpu.make_async_copy(matrix.at[0, rows], stage_v.at[k, half], recv_sem.at[1 + 2 * k + half]).start()

    def forward(k, half):
        arrived(stage_v.at[k, half], recv_sem.at[1 + 2 * k + half])
        rows = pl.ds(pl.multiple_of(c * 256 + half * 128, 128), 128)
        landing = dl_v.at[k, rows, pl.ds(pl.multiple_of(x * 128, 128), 128)]
        for i in OTHER_X:
            remote(stage_v.at[k, half], landing, send_sem.at[4], recv_sem.at[7 + 2 * k + half], at(dx=i)).start()
        pltpu.make_async_copy(stage_v.at[k, half], landing, recv_sem.at[7 + 2 * k + half]).start()

    def to_mate(ref, i):
        remote(ref, ref, t_send.at[i], t_recv.at[i], at(dc=1)).start()

    def share_matrix(k):
        for half in range(2):
            rows = pl.ds(pl.multiple_of(c * 256 + half * 128, 128), 128)
            arrived(dl_v.at[k, rows], recv_sem.at[7 + 2 * k + half])
            to_mate(dl_v.at[k, rows], 2 + 2 * k + half)

    def have_matrix(k):
        for half in range(2):
            arrived(dl_v.at[k, pl.ds(0, 128)], t_recv.at[2 + 2 * k + half])

    to_mate(beta_v.at[c], 1)

    @pl.when(d == 0)
    def _():
        for dy, dc, dx in SLAB:
            t = at(dy, dc, 0, dx)
            remote(res_v.at[rows_of(dx, dc)], first_v.at[x], send_sem.at[0], recv_sem.at[0], t).start()
        pltpu.make_async_copy(res_v.at[own_rows], first_v.at[x], recv_sem.at[0]).start()
        cut(0, 0)
        cut(0, 1)

    inv_columns = pl.ds(pl.multiple_of(c * 256, 256), 256)
    inv_landing = inv_v.at[pl.ds(pl.multiple_of(x * 128, 128), 128), inv_columns]
    for i in OTHER_X:
        remote(inverse, inv_landing, send_sem.at[2], recv_sem.at[5], at(dx=i)).start()
    pltpu.make_async_copy(inverse, inv_landing, recv_sem.at[5]).start()

    @pl.when(jnp.logical_and(d > 0, d < STEPS))
    def _():
        for dy, dc, dx in SLAB:
            if dy == 0:
                remote(res_v.at[rows_of(dx, dc)], base_v.at[x], send_sem.at[3], recv_sem.at[6], at(0, dc, 0, dx)).start()
        pltpu.make_async_copy(res_v.at[own_rows], base_v.at[x], recv_sem.at[6]).start()

    def pass_on(src, k):
        @pl.when(d > 0)
        def _():
            remote(src, passed.at[k], p_send.at[k], p_recv.at[k], (jnp.maximum(d - 1, 0), r)).start()

    def take(k):
        @pl.when(d < ND - 1)
        def _():
            arrived(passed.at[k], p_recv.at[k])

        return jnp.where(d < ND - 1, passed[k], 0.0)

    slot_rows = pl.ds(pl.multiple_of(x * NC * ROWS, NC * ROWS), NC * ROWS)

    def send_values(s):
        for part, where in enumerate((FAR, NEAR)):
            for dy, dc, dx in where:
                landing = c_all.at[s, c, (NY - dy) % NY, slot_rows]
                remote(c_own.at[s], landing, c_send.at[s], c_recv.at[s, part], at(dy, 0, 0, dx)).start()
        pltpu.make_async_copy(c_own.at[s], c_all.at[s, c, 0, slot_rows], c_recv.at[s, 1]).start()

    def share(s, part):
        arrived(mat_v.at[pl.ds(0, FAR_BLOCKS * BLOCK if part == 0 else NEAR_BLOCKS * BLOCK)], c_recv.at[s, part])
        for slots in (FAR_SLOTS,) if part == 0 else NEAR_SLOTS:
            piece = c_all.at[s, c, pl.ds(*slots)]
            remote(piece, piece, m_send.at[s], m_recv.at[s, part], at(dc=1)).start()

    def multiply(s, part, core):
        total = jnp.zeros((NX * ROWS, 128), F32)
        for first, slots in (FAR_SLOTS,) if part == 0 else NEAR_SLOTS:
            for slot in range(first, first + slots):
                for half, values in enumerate(halves(c_all[s, core, slot])):
                    at_row = (NC * lax.rem(y + slot, NY) + half) * 256
                    rows = pl.ds(pl.multiple_of(at_row, 256), 256)
                    total += jnp.dot(values.astype(BF16), mat_v[rows], preferred_element_type=F32)
        return total

    def product(s):
        share(s, 0)
        own = multiply(s, 0, c)
        share(s, 1)
        own += multiply(s, 1, c)
        other = jnp.zeros((NX * ROWS, 128), F32)
        for part, blocks in enumerate((FAR_BLOCKS, NEAR_BLOCKS)):
            arrived(mat_v.at[pl.ds(0, blocks * BLOCK)], m_recv.at[s, part])
            other += multiply(s, part, 1 - c)
        columns = [jnp.where(c == 0, *halves(c_all[s, core, 0])) for core in range(NC)]
        currents[s] = in_order(*columns, 256).astype(BF16)
        return in_order(jnp.where(c == 0, own, other), jnp.where(c == 0, other, own), 128)

    def side_by_side(blocks):
        return jnp.concatenate([blocks[i].astype(F32) for i in range(NX)], axis=1)

    arrived(inv_v.at[:, inv_columns], recv_sem.at[5])
    to_mate(inv_v.at[:, inv_columns], 0)
    arrived(first_v, recv_sem.at[0])
    residual = side_by_side(first_v)
    for s in range(STEPS):
        if s == 0:
            arrived(inv_v.at[:, inv_columns], t_recv.at[0])
        partial_sum = jnp.dot(residual.astype(BF16), inv_v[...], preferred_element_type=F32)
        zbuf[s, z] = stacked(partial_sum).astype(BF16)
        for i in LINE:
            remote(zbuf.at[s, z], zbuf.at[s, z], z_send.at[s], z_recv.at[s], at(dz=i)).start()
        if s == 0:
            forward(0, 0)
            forward(0, 1)

            @pl.when(d == 0)
            def _():
                left(mat_v.at[pl.ds(0, (ND - 1) * 256)], send_sem.at[1])
                pl.semaphore_signal(next_sem, inc=1, device_id=at(dc=1), device_id_type=MESH)

            @pl.when(d == 1)
            def _():
                pl.semaphore_wait(next_sem, 1)
                cut(1, 0)
                cut(1, 1)

            pass_on(history.at[0], 0)

            @pl.when(y < STEPS - 1)
            def _():
                arrived(base_v, recv_sem.at[6])

            arrived(beta_v.at[c], t_recv.at[1])
            beta_wide = jnp.concatenate([jnp.broadcast_to(beta_v[i], (ROWS, 256)) for i in range(NC)], axis=0)

        if s == 1:
            share_matrix(1)
            send_values(0)
        if s == 2:
            loads[4].wait()
            future[0] = product(0) + take(0)
            pass_on(future.at[0], 1)

        arrived(zbuf.at[s, pl.ds(0, NZ - 1)], z_recv.at[s])
        solved = zbuf[s, 0].astype(F32)
        for i in range(1, NZ):
            solved += zbuf[s, i].astype(F32)
        current = (solved / (1.0 + beta_wide * solved * solved)).astype(BF16)
        c_own[s] = current
        if s < STEPS - 1:
            if s == 0:
                share_matrix(0)
            have_matrix(s)
            wide = unstacked(current.astype(F32)).astype(BF16)
            part = -jnp.dot(wide, dl_v[0], preferred_element_type=F32)
            if s == 0:
                earlier = wide
            else:
                part -= jnp.dot(earlier, dl_v[1], preferred_element_type=F32)
            part += jnp.where(y == s, side_by_side(base_v), 0.0)
            xbuf[s, y] = stacked(part).astype(BF16)
            for i in LINE:
                remote(xbuf.at[s, y], xbuf.at[s, y], x_send.at[s], x_recv.at[s], at(i)).start()

        if s > 0:
            send_values(s)
        if s < STEPS - 1:
            if s == 0:
                forward(1, 0)
                forward(1, 1)
            arrived(xbuf.at[s, pl.ds(0, NY - 1)], x_recv.at[s])
            total = xbuf[s, 0].astype(F32)
            for i in range(1, NY):
                total += xbuf[s, i].astype(F32)
            residual = unstacked(total)

    future[1] = product(1)
    future[1] = future[1] + take(1)
    pass_on(future.at[1], 2)

    for s in range(STEPS):
        left(zbuf.at[s, pl.ds(0, NZ - 1)], z_send.at[s])
        if s < STEPS - 1:
            left(xbuf.at[s, pl.ds(0, NY - 1)], x_send.at[s])
            left(mat_v.at[pl.ds(0, len(CORE) * BLOCK)], c_send.at[s])
            left(c_all.at[s, c], m_send.at[s])

        @pl.when(d > 0)
        def _(s=s):
            left(passed.at[s], p_send.at[s])

    left(inv_v.at[pl.ds(0, (NX - 1) * 128), inv_columns], send_sem.at[2])
    left(inv_v.at[:, inv_columns], t_send.at[0])
    left(beta_v.at[c], t_send.at[1])
    for i in range(2, 6):
        left(dl_v.at[0, pl.ds(0, 128)], t_send.at[i])
    left(mat_v.at[pl.ds(0, 2 * (NX - 1) * 256)], send_sem.at[4])

    @pl.when(d == 0)
    def _():
        left(mat_v.at[pl.ds(0, len(SLAB) * 16)], send_sem.at[0])

    @pl.when(d == 1)
    def _():
        left(mat_v.at[pl.ds(0, (ND - 1) * 256)], send_sem.at[1])

    @pl.when(jnp.logical_and(d > 0, d < STEPS))
    def _():
        left(mat_v.at[pl.ds(0, (NX * NC - 1) * 16)], send_sem.at[3])

    total = product(2)
    carried[0] = total + take(2)
    left(mat_v.at[pl.ds(0, len(CORE) * BLOCK)], c_send.at[STEPS - 1])
    left(c_all.at[STEPS - 1, c], m_send.at[STEPS - 1])


def per_device(incident, onset, beta, inverse_block, delay_blocks, history_sum):
    hbm = pl.BlockSpec(memory_space=pltpu.HBM)
    vmem = pl.BlockSpec(memory_space=pltpu.VMEM)
    dma = pltpu.SemaphoreType.DMA
    steps = dma((STEPS,))
    return pl.pallas_call(
        kernel,
        out_shape=(
            pltpu.VMEM((STEPS, 64, 256), BF16),
            pltpu.VMEM((1, 64, 128), F32),
        ),
        in_specs=[hbm] * 6,
        out_specs=(vmem, vmem),
        scratch_shapes=[
            pltpu.SMEM((64,), jnp.int32),
            pltpu.VMEM((64, 128), BF16),
            pltpu.VMEM((64, 128), F32),
            pltpu.VMEM((4096, 128), BF16),
            pltpu.VMEM((512, 512), BF16),
            pltpu.VMEM((2, 512, 512), BF16),
            pltpu.VMEM((2, 2, 128, 128), BF16),
            pltpu.VMEM((NC, 1, 256), F32),
            pltpu.VMEM((NX, ROWS, 128), F32),
            pltpu.VMEM((64, 128), F32),
            pltpu.VMEM((NX, ROWS, 128), F32),
            pltpu.VMEM((STEPS, NZ, 16, 256), BF16),
            pltpu.VMEM((STEPS - 1, NY, 16, 256), BF16),
            pltpu.VMEM((STEPS, 16, 256), BF16),
            pltpu.VMEM((STEPS, NC, NY, 64, 256), BF16),
            pltpu.VMEM((STEPS, 64, 128), F32),
            pltpu.VMEM((STEPS - 1, 64, 128), F32),
            dma((5,)),
            dma((5,)),
            dma((11,)),
            dma((6,)),
            dma((6,)),
            *[steps] * 5,
            dma((STEPS, 2)),
            steps,
            dma((STEPS, 2)),
            *[steps] * 2,
            pltpu.SemaphoreType.REGULAR,
        ],
        compiler_params=pltpu.CompilerParams(
            collective_id=0, has_side_effects=True, vmem_limit_bytes=60 * 10**6
        ),
    )(incident, onset, beta.reshape(1, 256), inverse_block, delay_blocks, history_sum)


def solution(mesh):
    placed = (
        P(None, "row"),
        P(),
        P("delay"),
        P("row", "delay"),
        P("delay", None, "row"),
        P("delay", None, "row"),
    )
    return jax.shard_map(
        per_device,
        mesh=mesh,
        in_specs=placed,
        out_specs=(P(None, None, "delay"), P("delay", None, "row")),
        check_vma=False,
    )
```

time: 66.2 us -> 64.4 us (0.973)
  Pallas kernels: 64.2 us -> 62.4 us
    pallas_call x1, Pallas kernels: 64.2 us -> 62.4 us  [per_device(): pl.pallas_call(kernel, out_shape=(pltpu.VMEM((STEPS, 64, 256), BF16), plt...]
where the time goes in v5:
time: 64.4 us; the launch traced here: 64.3 us
  Pallas kernels  62.4 us (97%)
  local copies, waits for them, and re-layouts  1.26 us (2%)
    pallas_call x1, Pallas kernels, per_device(): pl.pallas_call(kernel, out_shape=(pltpu.VMEM((STEPS, 64, 256), BF16), plt...  62.4 us

profile of v5, /device:TPU:1, one launch (start us, length us, event | category | flops | bytes accessed | tf_op | source)
XLA Modules:
  0.0 64.3 jit_solution(1532003345534357722)
XLA Ops:
  0.6 62.4 %shard_map.77 = (bf16[3,64,256]{2,1,0:T(8,128)(2,1)S(1)}, f32[1,64,128]{2,1,0:T(8,128)S(1)}) custom-call(bf16[64,128]{1,0:T(8,128)(2,1)} %incident.1, s32[64]{0:T(128)} %onset.1, f32[1,256]{1,0:T(1,128)} %bitcast.1, bf16[128,256]{1,0:T(8,128)(2,1)} %inverse.1, bf16[1,4096,128]{2,1,0:T(8,128)(2,1)} %matrix.1, f32[1,64,128]{2,1,0:T(8,128)} %history.1), custom_call_target="tpu_custom_call" | custom-call | tf_op jit(solution)/shard_map/pallas_call | solution.py:344
  63.0 0.6 %copy.10 = bf16[3,64,256]{2,1,0:T(8,128)(2,1)} copy(bf16[3,64,256]{2,1,0:T(8,128)(2,1)S(1)} %get-tuple-element.2) | data formatting | bytes 196608
  63.7 0.6 copy.11

commit v6 on v5

--- a/solution.py
+++ b/solution.py
@@ -253,12 +253,14 @@
                 arrived(base_v, recv_sem.at[6])
 
             arrived(beta_v.at[c], t_recv.at[1])
+            share_matrix(0)
             beta_wide = jnp.concatenate([jnp.broadcast_to(beta_v[i], (ROWS, 256)) for i in range(NC)], axis=0)
 
         if s == 1:
+            send_values(0)
             share_matrix(1)
-            send_values(0)
         if s == 2:
+            send_values(1)
             loads[4].wait()
             future[0] = product(0) + take(0)
             pass_on(future.at[0], 1)
@@ -270,8 +272,6 @@
         current = (solved / (1.0 + beta_wide * solved * solved)).astype(BF16)
         c_own[s] = current
         if s < STEPS - 1:
-            if s == 0:
-                share_matrix(0)
             have_matrix(s)
             wide = unstacked(current.astype(F32)).astype(BF16)
             part = -jnp.dot(wide, dl_v[0], preferred_element_type=F32)
@@ -284,7 +284,7 @@
             for i in LINE:
                 remote(xbuf.at[s, y], xbuf.at[s, y], x_send.at[s], x_recv.at[s], at(i)).start()
 
-        if s > 0:
+        if s == STEPS - 1:
             send_values(s)
         if s < STEPS - 1:
             if s == 0:

time: 64.4 us -> 63.2 us (0.981)
  Pallas kernels: 62.4 us -> 61.2 us
    pallas_call x1, Pallas kernels: 62.4 us -> 61.2 us  [per_device(): pl.pallas_call(kernel, out_shape=(pltpu.VMEM((STEPS, 64, 256), BF16), plt...]
where the time goes in v6:
time: 63.2 us; the launch traced here: 63 us
  Pallas kernels  61.2 us (97%)
  local copies, waits for them, and re-layouts  1.26 us (2%)
  between operations  0.64 us (1%)
    pallas_call x1, Pallas kernels, per_device(): pl.pallas_call(kernel, out_shape=(pltpu.VMEM((STEPS, 64, 256), BF16), plt...  61.2 us

profile of v6, /device:TPU:1, one launch (start us, length us, event | category | flops | bytes accessed | tf_op | source)
XLA Modules:
  0.0 63.0 jit_solution(12517932764488773924)
XLA Ops:
  0.6 61.2 %shard_map.77 = (bf16[3,64,256]{2,1,0:T(8,128)(2,1)S(1)}, f32[1,64,128]{2,1,0:T(8,128)S(1)}) custom-call(bf16[64,128]{1,0:T(8,128)(2,1)} %incident.1, s32[64]{0:T(128)} %onset.1, f32[1,256]{1,0:T(1,128)} %bitcast.1, bf16[128,256]{1,0:T(8,128)(2,1)} %inverse.1, bf16[1,4096,128]{2,1,0:T(8,128)(2,1)} %matrix.1, f32[1,64,128]{2,1,0:T(8,128)} %history.1), custom_call_target="tpu_custom_call" | custom-call | tf_op jit(solution)/shard_map/pallas_call | solution.py:344
  61.8 0.6 %copy.10 = bf16[3,64,256]{2,1,0:T(8,128)(2,1)} copy(bf16[3,64,256]{2,1,0:T(8,128)(2,1)S(1)} %get-tuple-element.2) | data formatting | bytes 196608
  62.4 0.6 copy.11

commit v7 on v6

--- a/solution.py
+++ b/solution.py
@@ -246,7 +246,6 @@
                 cut(1, 0)
                 cut(1, 1)
 
-            pass_on(history.at[0], 0)
 
             @pl.when(y < STEPS - 1)
             def _():
@@ -257,6 +256,7 @@
             beta_wide = jnp.concatenate([jnp.broadcast_to(beta_v[i], (ROWS, 256)) for i in range(NC)], axis=0)
 
         if s == 1:
+            pass_on(history.at[0], 0)
             send_values(0)
             share_matrix(1)
         if s == 2:

time: 63.2 us -> 63.1 us (level)
  no operation moved by 1% of the time
where the time goes in v7:
time: 63.1 us; the launch traced here: 62.9 us
  Pallas kernels  61 us (97%)
  local copies, waits for them, and re-layouts  1.26 us (2%)
  between operations  0.64 us (1%)
    pallas_call x1, Pallas kernels, per_device(): pl.pallas_call(kernel, out_shape=(pltpu.VMEM((STEPS, 64, 256), BF16), plt...  61 us

profile of v7, /device:TPU:1, one launch (start us, length us, event | category | flops | bytes accessed | tf_op | source)
XLA Modules:
  0.0 62.9 jit_solution(2490041123683858047)
XLA Ops:
  0.6 61.0 %shard_map.77 = (bf16[3,64,256]{2,1,0:T(8,128)(2,1)S(1)}, f32[1,64,128]{2,1,0:T(8,128)S(1)}) custom-call(bf16[64,128]{1,0:T(8,128)(2,1)} %incident.1, s32[64]{0:T(128)} %onset.1, f32[1,256]{1,0:T(1,128)} %bitcast.1, bf16[128,256]{1,0:T(8,128)(2,1)} %inverse.1, bf16[1,4096,128]{2,1,0:T(8,128)(2,1)} %matrix.1, f32[1,64,128]{2,1,0:T(8,128)} %history.1), custom_call_target="tpu_custom_call" | custom-call | tf_op jit(solution)/shard_map/pallas_call | solution.py:344
  61.7 0.6 %copy.10 = bf16[3,64,256]{2,1,0:T(8,128)(2,1)} copy(bf16[3,64,256]{2,1,0:T(8,128)(2,1)S(1)} %get-tuple-element.2) | data formatting | bytes 196608
  62.3 0.6 copy.11
